TPU v7x, 128 devices: a whole 4x4x4 slice. The times are simulated.
128 devices in a mesh: group: 8 (over y, x_hi), member: 16 (over z, x_lo, core).
Axes of the slice: x: 4 (x_hi: 2, x_lo: 2; x = x_hi * 2 + x_lo), y: 4, z: 4, core: 2. Of those that a mesh axis runs over, the one named last changes fastest.
Arguments:
- embeddings: float32 [131072, 256], P(('group', 'member')), may hold values from -24 to 24, as said below
- operators: float32 [16, 256, 256], replicated, as said below
- plan: int32 [4], replicated, may hold values from 1 to 127, as said below
- relations: int32 [4, 1024], P(None, ('group', 'member')), may hold values from 0 to 15
Outputs:
- new_embeddings: float32 [131072, 256], P(('group', 'member'))
- new_operators: float32 [16, 256, 256], replicated
Inputs may be any that keep to these rules, and one draw needn't show every extreme that they name: The 4 values are distinct, so every round pairs distinct partitions two by two; both 1 and 127 occur in every plan. `embeddings`: rows are of order one; some rows may be several times larger. `operators`: each operator is the identity plus a dense full-rank part.
All inputs are finite; a program needn't handle non-finite values.
Results may differ from a plain program's by a relative error of at most 0.015.
The roundings to bfloat16 on the way count: a program that leaves them out, or rounds other values in their place, can miss the bound.
Values may be sent and summed in bfloat16 or wider, within the bound.
No kernel may reach another device: no remote copies, remote signals or barrier semaphores. Data moves between devices by JAX's collectives and lax.ppermute only.
A program may use at most 128 MiB of HBM per device.

v0:
```python
import math

import jax
import jax.numpy as jnp
from jax import lax
from jax.sharding import PartitionSpec as P

NEG = 1024
ROUNDS = 4


embed_rate = 1.0
operator_rate = 0.02


def from_partner(block, axis, apart):
    count = lax.axis_size(axis)
    route = []
    for low in range(count):
        high = low | 1 << apart
        if high != low and high < count:
            route += [(low, high), (high, low)]
    return lax.ppermute(block, axis, route)


def bit_sequence(bit_count):
    ordered = list(range(bit_count))
    return ordered


def fetch_partner(values, xor_mask):
    bit_count = lax.axis_size(("group", "member")).bit_length() - 1
    for bit_number in bit_sequence(bit_count):
        is_set = xor_mask >> bit_number & 1 == 1

        def fetch_moved(current, bit_number=bit_number):
            return from_partner(current, ("group", "member"), bit_number)

        def fetch_kept(current):
            return current

        values = lax.cond(is_set, fetch_moved, fetch_kept, values)
    return values


def return_grads(values, xor_mask):
    bit_count = lax.axis_size(("group", "member")).bit_length() - 1
    for bit_number in bit_sequence(bit_count):
        is_set = xor_mask >> bit_number & 1 == 1

        def return_moved(current, bit_number=bit_number):
            return from_partner(current, ("group", "member"), bit_number)

        def return_kept(current):
            return current

        values = lax.cond(is_set, return_moved, return_kept, values)
    return values


def shards(embeddings, operators, plan, relations):
    count_of_rows, feature = embeddings.shape
    relation_count = operators.shape[0]
    block_tiles = relations.shape[1]
    block_rows = count_of_rows // block_tiles
    neg_blocks = count_of_rows // NEG
    scale_of_scores = 1.0 / math.sqrt(feature)
    ops_flat = operators.astype(jnp.bfloat16).reshape(relation_count, feature * feature)
    identity = jnp.eye(NEG, dtype=jnp.float32)
    rel_index = jnp.arange(relation_count, dtype=jnp.int32)
    grad_total = jnp.zeros((relation_count, feature * feature), jnp.float32)
    embeds = embeddings
    for round_index in range(ROUNDS):
        xor_mask = plan[round_index]
        onehot = (relations[round_index][:, None] == rel_index[None, :]).astype(jnp.bfloat16)
        picked_rows = jnp.dot(onehot, ops_flat, preferred_element_type=jnp.float32).astype(
            jnp.bfloat16
        )
        picked_rows = picked_rows.reshape(block_tiles, feature, feature)
        own_rows = embeds.astype(jnp.bfloat16)
        partner = fetch_partner(own_rows, xor_mask)
        local_block_tiles = own_rows.reshape(block_tiles, block_rows, feature)
        query_rows = jnp.einsum(
            "rux,rxp->rup", local_block_tiles, picked_rows, preferred_element_type=jnp.float32
        ).astype(jnp.bfloat16)
        query_groupings = query_rows.reshape(neg_blocks, NEG, feature)
        partner_groupings = partner.reshape(neg_blocks, NEG, feature)
        score_matrix = (
            jnp.einsum(
                "mfn,mon->mfo",
                query_groupings,
                partner_groupings,
                preferred_element_type=jnp.float32,
            )
            * scale_of_scores
        )
        row_prob = jax.nn.softmax(score_matrix, axis=2)
        col_prob = jax.nn.softmax(score_matrix, axis=1)
        score_gradient = ((row_prob - identity + (col_prob - identity)) * scale_of_scores).astype(
            jnp.bfloat16
        )
        query_gradient = jnp.einsum(
            "rti,rie->rte", score_gradient, partner_groupings, preferred_element_type=jnp.float32
        ).astype(jnp.bfloat16)
        right_gradient = jnp.einsum(
            "lfv,lfh->lvh", score_gradient, query_groupings, preferred_element_type=jnp.float32
        ).astype(jnp.bfloat16)
        returned = return_grads(right_gradient.reshape(count_of_rows, feature), xor_mask)
        query_gradient_blocks = query_gradient.reshape(block_tiles, block_rows, feature)
        left_gradient = jnp.einsum(
            "jts,jus->jtu", query_gradient_blocks, picked_rows, preferred_element_type=jnp.float32
        ).reshape(count_of_rows, feature)
        block_gradient = jnp.einsum(
            "vmi,vmg->vig",
            local_block_tiles,
            query_gradient_blocks,
            preferred_element_type=jnp.float32,
        )
        block_gradient = block_gradient.reshape(block_tiles, feature * feature)
        grad_total = grad_total + jnp.dot(
            onehot.astype(jnp.float32).T, block_gradient, precision=lax.Precision.HIGHEST
        )
        embeds = embeds - embed_rate * (left_gradient + returned.astype(jnp.float32))
    summed = lax.psum(grad_total, ("group", "member"))
    new_operators = operators - operator_rate * summed.reshape(relation_count, feature, feature)
    return (embeds, new_operators)


def solution(mesh):
    return jax.shard_map(
        shards,
        mesh=mesh,
        in_specs=(P(("group", "member"), None), P(), P(), P(None, ("group", "member"))),
        out_specs=(P(("group", "member"), None), P()),
        check_vma=False,
    )
```

profile of v0, /device:TPU:1, one launch (start us, length us, event | category | flops | bytes accessed | tf_op | source)
XLA Modules:
  0.0 527.7 jit_solution(17318775482614017012)
XLA Ops:
  51.7 14.1 %conditional.75 = (bf16[1024,256]{1,0:T(8,128)(2,1)}) conditional(s32[]{:T(128)} %bitcast.20, bf16[1024,256]{1,0:T(8,128)(2,1)} %get-tuple-element.350, bf16[1024,256]{1,0:T(8,128)(2,1)} %get-tuple-element.350), branch_computations={%region_42.0_spmd, %region_43.0_spmd} | conditional | bytes 3145776 | solution.py:42
  53.1 12.0 %collective-permute-done.19 = bf16[1024,256]{1,0:T(8,128)(2,1)S(1)} collective-permute-done((bf16[1024,256]{1,0:T(8,128)(2,1)}, bf16[1024,256]{1,0:T(8,128)(2,1)S(1)}, u32[]{:S(2)}, u32[]{:S(2)}) %collective-permute-start.19) | collective-permute-done | bytes 524320 | tf_op jit(solution)/shard_map/cond/branch_1_fun/ppermute | solution.py:23
  81.0 13.3 %conditional.82 = (bf16[1024,256]{1,0:T(8,128)(2,1)}) conditional(s32[]{:T(128)} %bitcast.20, bf16[1024,256]{1,0:T(8,128)(2,1)} %get-tuple-element.357, bf16[1024,256]{1,0:T(8,128)(2,1)} %get-tuple-element.357), branch_computations={%region_60.0_spmd, %region_61.0_spmd} | conditional | bytes 3145776 | solution.py:57
  82.4 11.1 %collective-permute-done.26 = bf16[1024,256]{1,0:T(8,128)(2,1)S(1)} collective-permute-done((bf16[1024,256]{1,0:T(8,128)(2,1)}, bf16[1024,256]{1,0:T(8,128)(2,1)S(1)}, u32[]{:S(2)}, u32[]{:S(2)}) %collective-permute-start.26) | collective-permute-done | bytes 524320 | tf_op jit(solution)/shard_map/cond/branch_1_fun/ppermute | solution.py:23
  103.7 12.4 %conditional.85 = (bf16[1024,256]{1,0:T(8,128)(2,1)}) conditional(s32[]{:T(128)} %bitcast.37, bf16[1024,256]{1,0:T(8,128)(2,1)} %get-tuple-element.360, bf16[1024,256]{1,0:T(8,128)(2,1)} %get-tuple-element.360), branch_computations={%region_66.0_spmd, %region_67.0_spmd} | conditional | bytes 3145776 | solution.py:42
  105.1 10.2 %collective-permute-done.29 = bf16[1024,256]{1,0:T(8,128)(2,1)S(1)} collective-permute-done((bf16[1024,256]{1,0:T(8,128)(2,1)}, bf16[1024,256]{1,0:T(8,128)(2,1)S(1)}, u32[]{:S(2)}, u32[]{:S(2)}) %collective-permute-start.29) | collective-permute-done | bytes 524320 | tf_op jit(solution)/shard_map/cond/branch_1_fun/ppermute | solution.py:23
  116.1 12.9 %conditional.88 = (bf16[1024,256]{1,0:T(8,128)(2,1)}) conditional(s32[]{:T(128)} %bitcast.34, bf16[1024,256]{1,0:T(8,128)(2,1)} %get-tuple-element.363, bf16[1024,256]{1,0:T(8,128)(2,1)} %get-tuple-element.363), branch_computations={%region_72.0_spmd, %region_73.0_spmd} | conditional | bytes 3145776 | solution.py:42
  118.9 9.2 %collective-permute-done.32 = bf16[1024,256]{1,0:T(8,128)(2,1)S(1)} collective-permute-done((bf16[1024,256]{1,0:T(8,128)(2,1)}, bf16[1024,256]{1,0:T(8,128)(2,1)S(1)}, u32[]{:S(2)}, u32[]{:S(2)}) %collective-permute-start.32) | collective-permute-done | bytes 524320 | tf_op jit(solution)/shard_map/cond/branch_1_fun/ppermute | solution.py:23
  129.0 10.5 %conditional.89 = (bf16[1024,256]{1,0:T(8,128)(2,1)}) conditional(s32[]{:T(128)} %bitcast.33, bf16[1024,256]{1,0:T(8,128)(2,1)} %get-tuple-element.364, bf16[1024,256]{1,0:T(8,128)(2,1)} %get-tuple-element.364), branch_computations={%region_74.0_spmd, %region_75.0_spmd} | conditional | bytes 3145776 | solution.py:42
  130.3 8.3 %collective-permute-done.33 = bf16[1024,256]{1,0:T(8,128)(2,1)S(1)} collective-permute-done((bf16[1024,256]{1,0:T(8,128)(2,1)}, bf16[1024,256]{1,0:T(8,128)(2,1)S(1)}, u32[]{:S(2)}, u32[]{:S(2)}) %collective-permute-start.33) | collective-permute-done | bytes 524320 | tf_op jit(solution)/shard_map/cond/branch_1_fun/ppermute | solution.py:23
  139.4 14.3 %conditional.90 = (bf16[1024,256]{1,0:T(8,128)(2,1)}) conditional(s32[]{:T(128)} %bitcast.32, bf16[1024,256]{1,0:T(8,128)(2,1)} %get-tuple-element.365, bf16[1024,256]{1,0:T(8,128)(2,1)} %get-tuple-element.365), branch_computations={%region_76.0_spmd, %region_77.0_spmd} | conditional | bytes 3145776 | solution.py:42
  142.4 10.5 %collective-permute-done.34 = bf16[1024,256]{1,0:T(8,128)(2,1)S(1)} collective-permute-done((bf16[1024,256]{1,0:T(8,128)(2,1)}, bf16[1024,256]{1,0:T(8,128)(2,1)S(1)}, u32[]{:S(2)}, u32[]{:S(2)}) %collective-permute-start.34) | collective-permute-done | bytes 524320 | tf_op jit(solution)/shard_map/cond/branch_1_fun/ppermute | solution.py:23
  174.6 10.0 %conditional.92 = (bf16[1024,256]{1,0:T(8,128)(2,1)}) conditional(s32[]{:T(128)} %bitcast.37, bf16[1024,256]{1,0:T(8,128)(2,1)} %get-tuple-element.367, bf16[1024,256]{1,0:T(8,128)(2,1)} %get-tuple-element.367), branch_computations={%region_84.0_spmd, %region_85.0_spmd} | conditional | bytes 3145776 | solution.py:57
  175.9 8.0 %collective-permute-done.36 = bf16[1024,256]{1,0:T(8,128)(2,1)S(1)} collective-permute-done((bf16[1024,256]{1,0:T(8,128)(2,1)}, bf16[1024,256]{1,0:T(8,128)(2,1)S(1)}, u32[]{:S(2)}, u32[]{:S(2)}) %collective-permute-start.36) | collective-permute-done | bytes 524320 | tf_op jit(solution)/shard_map/cond/branch_1_fun/ppermute | solution.py:23
  184.6 14.3 %conditional.95 = (bf16[1024,256]{1,0:T(8,128)(2,1)}) conditional(s32[]{:T(128)} %bitcast.34, bf16[1024,256]{1,0:T(8,128)(2,1)} %get-tuple-element.370, bf16[1024,256]{1,0:T(8,128)(2,1)} %get-tuple-element.370), branch_computations={%region_90.0_spmd, %region_91.0_spmd} | conditional | bytes 3145776 | solution.py:57
  187.5 10.5 %collective-permute-done.39 = bf16[1024,256]{1,0:T(8,128)(2,1)S(1)} collective-permute-done((bf16[1024,256]{1,0:T(8,128)(2,1)}, bf16[1024,256]{1,0:T(8,128)(2,1)S(1)}, u32[]{:S(2)}, u32[]{:S(2)}) %collective-permute-start.39) | collective-permute-done | bytes 524320 | tf_op jit(solution)/shard_map/cond/branch_1_fun/ppermute | solution.py:23
  198.9 9.8 %conditional.96 = (bf16[1024,256]{1,0:T(8,128)(2,1)}) conditional(s32[]{:T(128)} %bitcast.33, bf16[1024,256]{1,0:T(8,128)(2,1)} %get-tuple-element.371, bf16[1024,256]{1,0:T(8,128)(2,1)} %get-tuple-element.371), branch_computations={%region_92.0_spmd, %region_93.0_spmd} | conditional | bytes 3145776 | solution.py:57
  198.9 9.0 %collective-permute-done.40 = bf16[1024,256]{1,0:T(8,128)(2,1)S(1)} collective-permute-done((bf16[1024,256]{1,0:T(8,128)(2,1)}, bf16[1024,256]{1,0:T(8,128)(2,1)S(1)}, u32[]{:S(2)}, u32[]{:S(2)}) %collective-permute-start.40) | collective-permute-done | bytes 524320 | tf_op jit(solution)/shard_map/cond/branch_1_fun/ppermute | solution.py:23
  208.7 13.4 %conditional.97 = (bf16[1024,256]{1,0:T(8,128)(2,1)}) conditional(s32[]{:T(128)} %bitcast.32, bf16[1024,256]{1,0:T(8,128)(2,1)} %get-tuple-element.372, bf16[1024,256]{1,0:T(8,128)(2,1)} %get-tuple-element.372), branch_computations={%region_94.0_spmd, %region_95.0_spmd} | conditional | bytes 3145776 | solution.py:57
  208.7 12.6 %collective-permute-done.41 = bf16[1024,256]{1,0:T(8,128)(2,1)S(1)} collective-permute-done((bf16[1024,256]{1,0:T(8,128)(2,1)}, bf16[1024,256]{1,0:T(8,128)(2,1)S(1)}, u32[]{:S(2)}, u32[]{:S(2)}) %collective-permute-start.41) | collective-permute-done | bytes 524320 | tf_op jit(solution)/shard_map/cond/branch_1_fun/ppermute | solution.py:23
  225.2 8.3 %conditional.98 = (bf16[1024,256]{1,0:T(8,128)(2,1)}) conditional(s32[]{:T(128)} %bitcast.51, bf16[1024,256]{1,0:T(8,128)(2,1)S(1)} %fusion.37, bf16[1024,256]{1,0:T(8,128)(2,1)S(1)} %fusion.37), branch_computations={%region_96.0_spmd, %region_97.0_spmd} | conditional | bytes 2097200 | solution.py:42
  225.2 6.4 %collective-permute-start.42 = (bf16[1024,256]{1,0:T(8,128)(2,1)S(1)}, bf16[1024,256]{1,0:T(8,128)(2,1)}, u32[]{:S(2)}, u32[]{:S(2)}) collective-permute-start(bf16[1024,256]{1,0:T(8,128)(2,1)S(1)} %param.85), channel_id=1, source_target_pairs={{0,1},{1,0},{2,3},{3,2},{4,5},{5,4},{6,7},{7,6},{8,9},{9,8},{10,11... | collective-permute-start | bytes 1572872 | tf_op jit(solution)/shard_map/cond/branch_1_fun/ppermute | solution.py:23
  233.9 16.7 %conditional.99 = (bf16[1024,256]{1,0:T(8,128)(2,1)}) conditional(s32[]{:T(128)} %bitcast.50, bf16[1024,256]{1,0:T(8,128)(2,1)} %get-tuple-element.374, bf16[1024,256]{1,0:T(8,128)(2,1)} %get-tuple-element.374), branch_computations={%region_98.0_spmd, %region_99.0_spmd} | conditional | bytes 3145776 | solution.py:42
  237.6 12.2 %collective-permute-done.43 = bf16[1024,256]{1,0:T(8,128)(2,1)S(1)} collective-permute-done((bf16[1024,256]{1,0:T(8,128)(2,1)}, bf16[1024,256]{1,0:T(8,128)(2,1)S(1)}, u32[]{:S(2)}, u32[]{:S(2)}) %collective-permute-start.43) | collective-permute-done | bytes 524320 | tf_op jit(solution)/shard_map/cond/branch_1_fun/ppermute | solution.py:23
  250.6 14.0 %conditional.100 = (bf16[1024,256]{1,0:T(8,128)(2,1)}) conditional(s32[]{:T(128)} %bitcast.49, bf16[1024,256]{1,0:T(8,128)(2,1)} %get-tuple-element.375, bf16[1024,256]{1,0:T(8,128)(2,1)} %get-tuple-element.375), branch_computations={%region_100.0_spmd, %region_101.0_spmd} | conditional | bytes 3145776 | solution.py:42
  252.3 11.5 %collective-permute-done.44 = bf16[1024,256]{1,0:T(8,128)(2,1)S(1)} collective-permute-done((bf16[1024,256]{1,0:T(8,128)(2,1)}, bf16[1024,256]{1,0:T(8,128)(2,1)S(1)}, u32[]{:S(2)}, u32[]{:S(2)}) %collective-permute-start.44) | collective-permute-done | bytes 524320 | tf_op jit(solution)/shard_map/cond/branch_1_fun/ppermute | solution.py:23
  264.6 14.8 %conditional.101 = (bf16[1024,256]{1,0:T(8,128)(2,1)}) conditional(s32[]{:T(128)} %bitcast.48, bf16[1024,256]{1,0:T(8,128)(2,1)} %get-tuple-element.376, bf16[1024,256]{1,0:T(8,128)(2,1)} %get-tuple-element.376), branch_computations={%region_102.0_spmd, %region_103.0_spmd} | conditional | bytes 3145776 | solution.py:42
  267.9 10.7 %collective-permute-done.45 = bf16[1024,256]{1,0:T(8,128)(2,1)S(1)} collective-permute-done((bf16[1024,256]{1,0:T(8,128)(2,1)}, bf16[1024,256]{1,0:T(8,128)(2,1)S(1)}, u32[]{:S(2)}, u32[]{:S(2)}) %collective-permute-start.45) | collective-permute-done | bytes 524320 | tf_op jit(solution)/shard_map/cond/branch_1_fun/ppermute | solution.py:23
  279.4 13.5 %conditional.102 = (bf16[1024,256]{1,0:T(8,128)(2,1)}) conditional(s32[]{:T(128)} %bitcast.47, bf16[1024,256]{1,0:T(8,128)(2,1)} %get-tuple-element.377, bf16[1024,256]{1,0:T(8,128)(2,1)} %get-tuple-element.377), branch_computations={%region_104.0_spmd, %region_105.0_spmd} | conditional | bytes 3145776 | solution.py:42
  281.1 11.0 %collective-permute-done.46 = bf16[1024,256]{1,0:T(8,128)(2,1)S(1)} collective-permute-done((bf16[1024,256]{1,0:T(8,128)(2,1)}, bf16[1024,256]{1,0:T(8,128)(2,1)S(1)}, u32[]{:S(2)}, u32[]{:S(2)}) %collective-permute-start.46) | collective-permute-done | bytes 524320 | tf_op jit(solution)/shard_map/cond/branch_1_fun/ppermute | solution.py:23
  292.9 11.1 %conditional.103 = (bf16[1024,256]{1,0:T(8,128)(2,1)}) conditional(s32[]{:T(128)} %bitcast.46, bf16[1024,256]{1,0:T(8,128)(2,1)} %get-tuple-element.378, bf16[1024,256]{1,0:T(8,128)(2,1)} %get-tuple-element.378), branch_computations={%region_106.0_spmd, %region_107.0_spmd} | conditional | bytes 3145776 | solution.py:42
  293.5 9.7 %collective-permute-done.47 = bf16[1024,256]{1,0:T(8,128)(2,1)S(1)} collective-permute-done((bf16[1024,256]{1,0:T(8,128)(2,1)}, bf16[1024,256]{1,0:T(8,128)(2,1)S(1)}, u32[]{:S(2)}, u32[]{:S(2)}) %collective-permute-start.47) | collective-permute-done | bytes 524320 | tf_op jit(solution)/shard_map/cond/branch_1_fun/ppermute | solution.py:23
  304.1 14.4 %conditional.104 = (bf16[1024,256]{1,0:T(8,128)(2,1)}) conditional(s32[]{:T(128)} %bitcast.45, bf16[1024,256]{1,0:T(8,128)(2,1)} %get-tuple-element.379, bf16[1024,256]{1,0:T(8,128)(2,1)} %get-tuple-element.379), branch_computations={%region_108.0_spmd, %region_109.0_spmd} | conditional | bytes 3145776 | solution.py:42
  307.3 10.2 %collective-permute-done.48 = bf16[1024,256]{1,0:T(8,128)(2,1)S(1)} collective-permute-done((bf16[1024,256]{1,0:T(8,128)(2,1)}, bf16[1024,256]{1,0:T(8,128)(2,1)S(1)}, u32[]{:S(2)}, u32[]{:S(2)}) %collective-permute-start.48) | collective-permute-done | bytes 524320 | tf_op jit(solution)/shard_map/cond/branch_1_fun/ppermute | solution.py:23
  352.7 6.6 %conditional.105 = (bf16[1024,256]{1,0:T(8,128)(2,1)}) conditional(s32[]{:T(128)} %bitcast.51, bf16[1024,256]{1,0:T(8,128)(2,1)} %convolution_convert_fusion.5, bf16[1024,256]{1,0:T(8,128)(2,1)} %convolution_convert_fusion.5), branch_computations={%region_114.0_spmd, %region_115.0_spmd} | conditional | bytes 3145776 | solution.py:57
  359.3 17.4 %conditional.106 = (bf16[1024,256]{1,0:T(8,128)(2,1)}) conditional(s32[]{:T(128)} %bitcast.50, bf16[1024,256]{1,0:T(8,128)(2,1)} %get-tuple-element.381, bf16[1024,256]{1,0:T(8,128)(2,1)} %get-tuple-element.381), branch_computations={%region_116.0_spmd, %region_117.0_spmd} | conditional | bytes 3145776 | solution.py:57
  359.4 16.5 %collective-permute-done.50 = bf16[1024,256]{1,0:T(8,128)(2,1)S(1)} collective-permute-done((bf16[1024,256]{1,0:T(8,128)(2,1)}, bf16[1024,256]{1,0:T(8,128)(2,1)S(1)}, u32[]{:S(2)}, u32[]{:S(2)}) %collective-permute-start.50) | collective-permute-done | bytes 524320 | tf_op jit(solution)/shard_map/cond/branch_1_fun/ppermute | solution.py:23
  376.7 15.8 %conditional.107 = (bf16[1024,256]{1,0:T(8,128)(2,1)}) conditional(s32[]{:T(128)} %bitcast.49, bf16[1024,256]{1,0:T(8,128)(2,1)} %get-tuple-element.382, bf16[1024,256]{1,0:T(8,128)(2,1)} %get-tuple-element.382), branch_computations={%region_118.0_spmd, %region_119.0_spmd} | conditional | bytes 3145776 | solution.py:57
  378.4 13.3 %collective-permute-done.51 = bf16[1024,256]{1,0:T(8,128)(2,1)S(1)} collective-permute-done((bf16[1024,256]{1,0:T(8,128)(2,1)}, bf16[1024,256]{1,0:T(8,128)(2,1)S(1)}, u32[]{:S(2)}, u32[]{:S(2)}) %collective-permute-start.51) | collective-permute-done | bytes 524320 | tf_op jit(solution)/shard_map/cond/branch_1_fun/ppermute | solution.py:23
  392.5 17.4 %conditional.108 = (bf16[1024,256]{1,0:T(8,128)(2,1)}) conditional(s32[]{:T(128)} %bitcast.48, bf16[1024,256]{1,0:T(8,128)(2,1)} %get-tuple-element.383, bf16[1024,256]{1,0:T(8,128)(2,1)} %get-tuple-element.383), branch_computations={%region_120.0_spmd, %region_121.0_spmd} | conditional | bytes 3145776 | solution.py:57
  396.0 13.1 %collective-permute-done.52 = bf16[1024,256]{1,0:T(8,128)(2,1)S(1)} collective-permute-done((bf16[1024,256]{1,0:T(8,128)(2,1)}, bf16[1024,256]{1,0:T(8,128)(2,1)S(1)}, u32[]{:S(2)}, u32[]{:S(2)}) %collective-permute-start.52) | collective-permute-done | bytes 524320 | tf_op jit(solution)/shard_map/cond/branch_1_fun/ppermute | solution.py:23
  409.9 14.5 %conditional.109 = (bf16[1024,256]{1,0:T(8,128)(2,1)}) conditional(s32[]{:T(128)} %bitcast.47, bf16[1024,256]{1,0:T(8,128)(2,1)} %get-tuple-element.384, bf16[1024,256]{1,0:T(8,128)(2,1)} %get-tuple-element.384), branch_computations={%region_122.0_spmd, %region_123.0_spmd} | conditional | bytes 3145776 | solution.py:57
  409.9 13.7 %collective-permute-done.53 = bf16[1024,256]{1,0:T(8,128)(2,1)S(1)} collective-permute-done((bf16[1024,256]{1,0:T(8,128)(2,1)}, bf16[1024,256]{1,0:T(8,128)(2,1)S(1)}, u32[]{:S(2)}, u32[]{:S(2)}) %collective-permute-start.53) | collective-permute-done | bytes 524320 | tf_op jit(solution)/shard_map/cond/branch_1_fun/ppermute | solution.py:23
  424.4 12.2 %conditional.110 = (bf16[1024,256]{1,0:T(8,128)(2,1)}) conditional(s32[]{:T(128)} %bitcast.46, bf16[1024,256]{1,0:T(8,128)(2,1)} %get-tuple-element.385, bf16[1024,256]{1,0:T(8,128)(2,1)} %get-tuple-element.385), branch_computations={%region_124.0_spmd, %region_125.0_spmd} | conditional | bytes 3145776 | solution.py:57
  424.4 11.4 %collective-permute-done.54 = bf16[1024,256]{1,0:T(8,128)(2,1)S(1)} collective-permute-done((bf16[1024,256]{1,0:T(8,128)(2,1)}, bf16[1024,256]{1,0:T(8,128)(2,1)S(1)}, u32[]{:S(2)}, u32[]{:S(2)}) %collective-permute-start.54) | collective-permute-done | bytes 524320 | tf_op jit(solution)/shard_map/cond/branch_1_fun/ppermute | solution.py:23
  436.6 13.0 %conditional.111 = (bf16[1024,256]{1,0:T(8,128)(2,1)}) conditional(s32[]{:T(128)} %bitcast.45, bf16[1024,256]{1,0:T(8,128)(2,1)} %get-tuple-element.386, bf16[1024,256]{1,0:T(8,128)(2,1)} %get-tuple-element.386), branch_computations={%region_126.0_spmd, %region_127.0_spmd} | conditional | bytes 3145776 | solution.py:57
  438.4 10.3 %collective-permute-done.55 = bf16[1024,256]{1,0:T(8,128)(2,1)S(1)} collective-permute-done((bf16[1024,256]{1,0:T(8,128)(2,1)}, bf16[1024,256]{1,0:T(8,128)(2,1)S(1)}, u32[]{:S(2)}, u32[]{:S(2)}) %collective-permute-start.55) | collective-permute-done | bytes 524320 | tf_op jit(solution)/shard_map/cond/branch_1_fun/ppermute | solution.py:23
  453.6 59.1 %all-reduce.2.cloned.1.call-done = f32[16,65536]{1,0:T(8,128)} async-done(((f32[16,65536]{1,0:T(8,128)}), f32[16,65536]{1,0:T(8,128)}) %all-reduce.2.cloned.1.call-update) | async-done | bytes 4194320 | tf_op jit(solution)/shard_map/psum | solution.py:124
  (202 shorter events, 191.5 us)
Async XLA Ops:
  7.2 505.6 %all-reduce.2.cloned.1.call-start = ((), (), s32[]{:S(2)}) async-start(), calls=%async_computation | async-start | bytes 8388608 | tf_op jit(solution)/shard_map/psum | solution.py:124
  19.0 4.4 copy-start.10
  19.0 3.8 copy-start.25
  23.4 5.4 %copy-start.6 = (bf16[8,65536]{1,0:T(8,128)(2,1)}, bf16[8,65536]{1,0:T(8,128)(2,1)S(1)}, u32[]{:S(2)}) copy-start(bf16[8,65536]{1,0:T(8,128)(2,1)S(1)} %convolution_convert_fusion.3) | copy-start | bytes 3145732
  23.4 3.2 collective-permute-start
  32.7 2.7 copy-start.22
  39.6 2.1 collective-permute-start.7
  42.5 3.8 copy-start.2
  51.7 13.3 %collective-permute-start.19 = (bf16[1024,256]{1,0:T(8,128)(2,1)}, bf16[1024,256]{1,0:T(8,128)(2,1)S(1)}, u32[]{:S(2)}, u32[]{:S(2)}) collective-permute-start(bf16[1024,256]{1,0:T(8,128)(2,1)} %param.39), channel_id=1, source_target_pairs={{0,32},{32,0},{1,33},{33,1},{2,34},{34,2},{3,35},{35,3},{4,36},{36... | collective-permute-start | bytes 1572872 | tf_op jit(solution)/shard_map/cond/branch_1_fun/ppermute | solution.py:23
  69.8 2.7 copy-start.23
  81.0 12.5 %collective-permute-start.26 = (bf16[1024,256]{1,0:T(8,128)(2,1)}, bf16[1024,256]{1,0:T(8,128)(2,1)S(1)}, u32[]{:S(2)}, u32[]{:S(2)}) collective-permute-start(bf16[1024,256]{1,0:T(8,128)(2,1)} %param.53), channel_id=1, source_target_pairs={{0,32},{32,0},{1,33},{33,1},{2,34},{34,2},{3,35},{35,3},{4,36},{36... | collective-permute-start | bytes 1572872 | tf_op jit(solution)/shard_map/cond/branch_1_fun/ppermute | solution.py:23
  94.3 3.5 copy-start.5
  94.3 3.5 copy-start.24
  103.7 11.6 %collective-permute-start.29 = (bf16[1024,256]{1,0:T(8,128)(2,1)}, bf16[1024,256]{1,0:T(8,128)(2,1)S(1)}, u32[]{:S(2)}, u32[]{:S(2)}) collective-permute-start(bf16[1024,256]{1,0:T(8,128)(2,1)} %param.59), channel_id=1, source_target_pairs={{0,2},{2,0},{1,3},{3,1},{4,6},{6,4},{5,7},{7,5},{8,10},{10,8},{9,1... | collective-permute-start | bytes 1572872 | tf_op jit(solution)/shard_map/cond/branch_1_fun/ppermute | solution.py:23
  116.1 12.1 %collective-permute-start.32 = (bf16[1024,256]{1,0:T(8,128)(2,1)}, bf16[1024,256]{1,0:T(8,128)(2,1)S(1)}, u32[]{:S(2)}, u32[]{:S(2)}) collective-permute-start(bf16[1024,256]{1,0:T(8,128)(2,1)} %param.65), channel_id=1, source_target_pairs={{0,16},{16,0},{1,17},{17,1},{2,18},{18,2},{3,19},{19,3},{4,20},{20... | collective-permute-start | bytes 1572872 | tf_op jit(solution)/shard_map/cond/branch_1_fun/ppermute | solution.py:23
  129.0 9.7 %collective-permute-start.33 = (bf16[1024,256]{1,0:T(8,128)(2,1)}, bf16[1024,256]{1,0:T(8,128)(2,1)S(1)}, u32[]{:S(2)}, u32[]{:S(2)}) collective-permute-start(bf16[1024,256]{1,0:T(8,128)(2,1)} %param.67), channel_id=1, source_target_pairs={{0,32},{32,0},{1,33},{33,1},{2,34},{34,2},{3,35},{35,3},{4,36},{36... | collective-permute-start | bytes 1572872 | tf_op jit(solution)/shard_map/cond/branch_1_fun/ppermute | solution.py:23
  139.4 13.5 %collective-permute-start.34 = (bf16[1024,256]{1,0:T(8,128)(2,1)}, bf16[1024,256]{1,0:T(8,128)(2,1)S(1)}, u32[]{:S(2)}, u32[]{:S(2)}) collective-permute-start(bf16[1024,256]{1,0:T(8,128)(2,1)} %param.69), channel_id=1, source_target_pairs={{0,64},{64,0},{1,65},{65,1},{2,66},{66,2},{3,67},{67,3},{4,68},{68... | collective-permute-start | bytes 1572872 | tf_op jit(solution)/shard_map/cond/branch_1_fun/ppermute | solution.py:23
  161.8 6.8 %copy-start.11 = (bf16[1024,256]{1,0:T(8,128)(2,1)S(1)}, bf16[1024,256]{1,0:T(8,128)(2,1)}, u32[]{:S(2)}) copy-start(bf16[1024,256]{1,0:T(8,128)(2,1)} %copy-done.10) | copy-start | bytes 1572868
  161.8 6.8 %copy-start.17 = (bf16[1024,256]{1,0:T(8,128)(2,1)S(1)}, bf16[1024,256]{1,0:T(8,128)(2,1)}, u32[]{:S(2)}) copy-start(bf16[1024,256]{1,0:T(8,128)(2,1)} %convolution_convert_fusion.15) | copy-start | bytes 1572868
  161.8 8.7 %copy-start.13 = (bf16[1024,256]{1,0:T(8,128)(2,1)S(1)}, bf16[1024,256]{1,0:T(8,128)(2,1)}, u32[]{:S(2)}) copy-start(bf16[1024,256]{1,0:T(8,128)(2,1)} %copy-done.12) | copy-start | bytes 1572868
  161.8 8.7 %copy-start.18 = (bf16[1024,256]{1,0:T(8,128)(2,1)S(1)}, bf16[1024,256]{1,0:T(8,128)(2,1)}, u32[]{:S(2)}) copy-start(bf16[1024,256]{1,0:T(8,128)(2,1)} %convolution_convert_fusion.12) | copy-start | bytes 1572868
  163.7 8.6 %copy-start.7 = (bf16[8,65536]{1,0:T(8,128)(2,1)S(1)}, bf16[8,65536]{1,0:T(8,128)(2,1)}, u32[]{:S(2)}) copy-start(bf16[8,65536]{1,0:T(8,128)(2,1)} %convolution_convert_fusion.1) | copy-start | bytes 3145732
  168.6 4.1 copy-start.15
  174.6 9.2 %collective-permute-start.36 = (bf16[1024,256]{1,0:T(8,128)(2,1)}, bf16[1024,256]{1,0:T(8,128)(2,1)S(1)}, u32[]{:S(2)}, u32[]{:S(2)}) collective-permute-start(bf16[1024,256]{1,0:T(8,128)(2,1)} %param.73), channel_id=1, source_target_pairs={{0,2},{2,0},{1,3},{3,1},{4,6},{6,4},{5,7},{7,5},{8,10},{10,8},{9,1... | collective-permute-start | bytes 1572872 | tf_op jit(solution)/shard_map/cond/branch_1_fun/ppermute | solution.py:23
  184.6 13.5 %collective-permute-start.39 = (bf16[1024,256]{1,0:T(8,128)(2,1)}, bf16[1024,256]{1,0:T(8,128)(2,1)S(1)}, u32[]{:S(2)}, u32[]{:S(2)}) collective-permute-start(bf16[1024,256]{1,0:T(8,128)(2,1)} %param.79), channel_id=1, source_target_pairs={{0,16},{16,0},{1,17},{17,1},{2,18},{18,2},{3,19},{19,3},{4,20},{20... | collective-permute-start | bytes 1572872 | tf_op jit(solution)/shard_map/cond/branch_1_fun/ppermute | solution.py:23
  198.9 9.0 %collective-permute-start.40 = (bf16[1024,256]{1,0:T(8,128)(2,1)}, bf16[1024,256]{1,0:T(8,128)(2,1)S(1)}, u32[]{:S(2)}, u32[]{:S(2)}) collective-permute-start(bf16[1024,256]{1,0:T(8,128)(2,1)} %param.81), channel_id=1, source_target_pairs={{0,32},{32,0},{1,33},{33,1},{2,34},{34,2},{3,35},{35,3},{4,36},{36... | collective-permute-start | bytes 1572872 | tf_op jit(solution)/shard_map/cond/branch_1_fun/ppermute | solution.py:23
  208.7 12.6 %collective-permute-start.41 = (bf16[1024,256]{1,0:T(8,128)(2,1)}, bf16[1024,256]{1,0:T(8,128)(2,1)S(1)}, u32[]{:S(2)}, u32[]{:S(2)}) collective-permute-start(bf16[1024,256]{1,0:T(8,128)(2,1)} %param.83), channel_id=1, source_target_pairs={{0,64},{64,0},{1,65},{65,1},{2,66},{66,2},{3,67},{67,3},{4,68},{68... | collective-permute-start | bytes 1572872 | tf_op jit(solution)/shard_map/cond/branch_1_fun/ppermute | solution.py:23
  223.6 9.9 %copy-start.3 = (bf16[8,65536]{1,0:T(8,128)(2,1)S(1)}, bf16[8,65536]{1,0:T(8,128)(2,1)}, u32[]{:S(2)}) copy-start(bf16[8,65536]{1,0:T(8,128)(2,1)} %convolution_convert_fusion) | copy-start | bytes 3145732
  225.2 8.1 %collective-permute-start.42 = (bf16[1024,256]{1,0:T(8,128)(2,1)S(1)}, bf16[1024,256]{1,0:T(8,128)(2,1)}, u32[]{:S(2)}, u32[]{:S(2)}) collective-permute-start(bf16[1024,256]{1,0:T(8,128)(2,1)S(1)} %param.85), channel_id=1, source_target_pairs={{0,1},{1,0},{2,3},{3,2},{4,5},{5,4},{6,7},{7,6},{8,9},{9,8},{10,11... | collective-permute-start | bytes 1572872 | tf_op jit(solution)/shard_map/cond/branch_1_fun/ppermute | solution.py:23
  233.9 86.4 %copy-start.20 = (bf16[8,128,256]{2,1,0:T(8,128)(2,1)}, bf16[8,128,256]{2,1,0:T(8,128)(2,1)S(1)}, u32[]{:S(2)}) copy-start(bf16[8,128,256]{2,1,0:T(8,128)(2,1)S(1)} %convolution_convert_fusion.7) | copy-start | bytes 1572868
  233.9 15.9 %collective-permute-start.43 = (bf16[1024,256]{1,0:T(8,128)(2,1)}, bf16[1024,256]{1,0:T(8,128)(2,1)S(1)}, u32[]{:S(2)}, u32[]{:S(2)}) collective-permute-start(bf16[1024,256]{1,0:T(8,128)(2,1)} %param.87), channel_id=1, source_target_pairs={{0,2},{2,0},{1,3},{3,1},{4,6},{6,4},{5,7},{7,5},{8,10},{10,8},{9,1... | collective-permute-start | bytes 1572872 | tf_op jit(solution)/shard_map/cond/branch_1_fun/ppermute | solution.py:23
  250.6 13.2 %collective-permute-start.44 = (bf16[1024,256]{1,0:T(8,128)(2,1)}, bf16[1024,256]{1,0:T(8,128)(2,1)S(1)}, u32[]{:S(2)}, u32[]{:S(2)}) collective-permute-start(bf16[1024,256]{1,0:T(8,128)(2,1)} %param.89), channel_id=1, source_target_pairs={{0,4},{4,0},{1,5},{5,1},{2,6},{6,2},{3,7},{7,3},{8,12},{12,8},{9,1... | collective-permute-start | bytes 1572872 | tf_op jit(solution)/shard_map/cond/branch_1_fun/ppermute | solution.py:23
  264.6 13.9 %collective-permute-start.45 = (bf16[1024,256]{1,0:T(8,128)(2,1)}, bf16[1024,256]{1,0:T(8,128)(2,1)S(1)}, u32[]{:S(2)}, u32[]{:S(2)}) collective-permute-start(bf16[1024,256]{1,0:T(8,128)(2,1)} %param.91), channel_id=1, source_target_pairs={{0,8},{8,0},{1,9},{9,1},{2,10},{10,2},{3,11},{11,3},{4,12},{12,4},... | collective-permute-start | bytes 1572872 | tf_op jit(solution)/shard_map/cond/branch_1_fun/ppermute | solution.py:23
  279.4 12.7 %collective-permute-start.46 = (bf16[1024,256]{1,0:T(8,128)(2,1)}, bf16[1024,256]{1,0:T(8,128)(2,1)S(1)}, u32[]{:S(2)}, u32[]{:S(2)}) collective-permute-start(bf16[1024,256]{1,0:T(8,128)(2,1)} %param.93), channel_id=1, source_target_pairs={{0,16},{16,0},{1,17},{17,1},{2,18},{18,2},{3,19},{19,3},{4,20},{20... | collective-permute-start | bytes 1572872 | tf_op jit(solution)/shard_map/cond/branch_1_fun/ppermute | solution.py:23
  292.9 10.3 %collective-permute-start.47 = (bf16[1024,256]{1,0:T(8,128)(2,1)}, bf16[1024,256]{1,0:T(8,128)(2,1)S(1)}, u32[]{:S(2)}, u32[]{:S(2)}) collective-permute-start(bf16[1024,256]{1,0:T(8,128)(2,1)} %param.95), channel_id=1, source_target_pairs={{0,32},{32,0},{1,33},{33,1},{2,34},{34,2},{3,35},{35,3},{4,36},{36... | collective-permute-start | bytes 1572872 | tf_op jit(solution)/shard_map/cond/branch_1_fun/ppermute | solution.py:23
  304.1 13.5 %collective-permute-start.48 = (bf16[1024,256]{1,0:T(8,128)(2,1)}, bf16[1024,256]{1,0:T(8,128)(2,1)S(1)}, u32[]{:S(2)}, u32[]{:S(2)}) collective-permute-start(bf16[1024,256]{1,0:T(8,128)(2,1)} %param.97), channel_id=1, source_target_pairs={{0,64},{64,0},{1,65},{65,1},{2,66},{66,2},{3,67},{67,3},{4,68},{68... | collective-permute-start | bytes 1572872 | tf_op jit(solution)/shard_map/cond/branch_1_fun/ppermute | solution.py:23
  328.0 10.8 %copy-start.19 = (bf16[1024,256]{1,0:T(8,128)(2,1)}, bf16[1024,256]{1,0:T(8,128)(2,1)S(1)}, u32[]{:S(2)}) copy-start(bf16[1024,256]{1,0:T(8,128)(2,1)S(1)} %convolution_convert_fusion.6) | copy-start | bytes 1572868
  334.3 1.9 copy-start.8
  334.4 3.2 copy-start.9
  352.7 5.8 %collective-permute-start.49 = (bf16[1024,256]{1,0:T(8,128)(2,1)}, bf16[1024,256]{1,0:T(8,128)(2,1)S(1)}, u32[]{:S(2)}, u32[]{:S(2)}) collective-permute-start(bf16[1024,256]{1,0:T(8,128)(2,1)} %param.99), channel_id=1, source_target_pairs={{0,1},{1,0},{2,3},{3,2},{4,5},{5,4},{6,7},{7,6},{8,9},{9,8},{10,11... | collective-permute-start | bytes 1572872 | tf_op jit(solution)/shard_map/cond/branch_1_fun/ppermute | solution.py:23
  359.3 16.6 %collective-permute-start.50 = (bf16[1024,256]{1,0:T(8,128)(2,1)}, bf16[1024,256]{1,0:T(8,128)(2,1)S(1)}, u32[]{:S(2)}, u32[]{:S(2)}) collective-permute-start(bf16[1024,256]{1,0:T(8,128)(2,1)} %param.101), channel_id=1, source_target_pairs={{0,2},{2,0},{1,3},{3,1},{4,6},{6,4},{5,7},{7,5},{8,10},{10,8},{9,1... | collective-permute-start | bytes 1572872 | tf_op jit(solution)/shard_map/cond/branch_1_fun/ppermute | solution.py:23
  376.7 74.4 %copy-start.1 = (f32[1024,256]{1,0:T(8,128)S(1)}, f32[1024,256]{1,0:T(8,128)}, u32[]{:S(2)}) copy-start(f32[1024,256]{1,0:T(8,128)} %get-tuple-element.315) | copy-start | bytes 3145732
  376.7 14.9 %collective-permute-start.51 = (bf16[1024,256]{1,0:T(8,128)(2,1)}, bf16[1024,256]{1,0:T(8,128)(2,1)S(1)}, u32[]{:S(2)}, u32[]{:S(2)}) collective-permute-start(bf16[1024,256]{1,0:T(8,128)(2,1)} %param.103), channel_id=1, source_target_pairs={{0,4},{4,0},{1,5},{5,1},{2,6},{6,2},{3,7},{7,3},{8,12},{12,8},{9,1... | collective-permute-start | bytes 1572872 | tf_op jit(solution)/shard_map/cond/branch_1_fun/ppermute | solution.py:23
  392.5 16.5 %collective-permute-start.52 = (bf16[1024,256]{1,0:T(8,128)(2,1)}, bf16[1024,256]{1,0:T(8,128)(2,1)S(1)}, u32[]{:S(2)}, u32[]{:S(2)}) collective-permute-start(bf16[1024,256]{1,0:T(8,128)(2,1)} %param.105), channel_id=1, source_target_pairs={{0,8},{8,0},{1,9},{9,1},{2,10},{10,2},{3,11},{11,3},{4,12},{12,4},... | collective-permute-start | bytes 1572872 | tf_op jit(solution)/shard_map/cond/branch_1_fun/ppermute | solution.py:23
  409.9 13.7 %collective-permute-start.53 = (bf16[1024,256]{1,0:T(8,128)(2,1)}, bf16[1024,256]{1,0:T(8,128)(2,1)S(1)}, u32[]{:S(2)}, u32[]{:S(2)}) collective-permute-start(bf16[1024,256]{1,0:T(8,128)(2,1)} %param.107), channel_id=1, source_target_pairs={{0,16},{16,0},{1,17},{17,1},{2,18},{18,2},{3,19},{19,3},{4,20},{20... | collective-permute-start | bytes 1572872 | tf_op jit(solution)/shard_map/cond/branch_1_fun/ppermute | solution.py:23
  424.4 11.4 %collective-permute-start.54 = (bf16[1024,256]{1,0:T(8,128)(2,1)}, bf16[1024,256]{1,0:T(8,128)(2,1)S(1)}, u32[]{:S(2)}, u32[]{:S(2)}) collective-permute-start(bf16[1024,256]{1,0:T(8,128)(2,1)} %param.109), channel_id=1, source_target_pairs={{0,32},{32,0},{1,33},{33,1},{2,34},{34,2},{3,35},{35,3},{4,36},{36... | collective-permute-start | bytes 1572872 | tf_op jit(solution)/shard_map/cond/branch_1_fun/ppermute | solution.py:23
  436.6 12.2 %collective-permute-start.55 = (bf16[1024,256]{1,0:T(8,128)(2,1)}, bf16[1024,256]{1,0:T(8,128)(2,1)S(1)}, u32[]{:S(2)}, u32[]{:S(2)}) collective-permute-start(bf16[1024,256]{1,0:T(8,128)(2,1)} %param.111), channel_id=1, source_target_pairs={{0,64},{64,0},{1,65},{65,1},{2,66},{66,2},{3,67},{67,3},{4,68},{68... | collective-permute-start | bytes 1572872 | tf_op jit(solution)/shard_map/cond/branch_1_fun/ppermute | solution.py:23
  515.3 2.2 copy-start
  (5 other events, 5.4 us)
Sparse Core Ops, SparseCore 0:
  348.6 164.0 all-reduce.1
where the time goes:
time: 537 us; the launch traced here: 528 us
  waiting for transfers between devices  311 us (58%)
  matrix products  57.7 us (11%)
  starting transfers between devices  49.1 us (9%)
  local copies, waits for them, and re-layouts  40.1 us (7%)
  other arithmetic  35.8 us (7%)
  between operations  33 us (6%)
    ppermute x26, waiting for transfers between devices, from_partner(): return lax.ppermute(block, axis, route)  252 us
    psum x1, waiting for transfers between devices, shards(): summed = lax.psum(grad_total, ('group', 'member'))  59.1 us
    ppermute x26, starting transfers between devices, from_partner(): return lax.ppermute(block, axis, route)  49.1 us
    cond x26, local copies, waits for them, and re-layouts  21.2 us
    unnamed x58, local copies, waits for them, and re-layouts  13.8 us
    convert_element_type x4, other arithmetic, shards(): ((row_prob - identity + (col_prob - identity)) * scale_of_scores).astype(...  10.8 us
  transfers between devices with their start and end apart: 27, of which 27 were waited for; matrix products, arithmetic and copies ran while one was open for 2% of the time, Pallas kernels for 0%

commit v1 on v0

v1 whole, which is shorter than its diff:
```python
import functools
import math

import jax
import jax.numpy as jnp
from jax import lax
from jax.experimental import pallas as pl
from jax.experimental.pallas import tpu as pltpu
from jax.sharding import PartitionSpec as P

ROUNDS = 4
AXES = ("group", "member")
CHUNK = 256
F32 = jnp.float32
BF16 = jnp.bfloat16

embed_rate = 1.0
operator_rate = 0.02


def dot_nt(a, b):
    return lax.dot_general(a, b, (((1,), (1,)), ((), ())), preferred_element_type=F32)


def dot_nn(a, b):
    return lax.dot_general(a, b, (((1,), (0,)), ((), ())), preferred_element_type=F32)


def dot_tn(a, b):
    return lax.dot_general(a, b, (((0,), (0,)), ((), ())), preferred_element_type=F32)


def two_way_gradient(x_ref, y_ref, s_ref, emit):
    rows, width = x_ref.shape
    chunks = rows // CHUNK
    scale = 1.0 / math.sqrt(width)
    in_bits = scale * math.log2(math.e)
    shift = -math.log2(scale)
    row_norm = []
    col_max = col_sum = None
    for i in range(chunks):
        block = pl.ds(i * CHUNK, CHUNK)
        s = dot_nt(x_ref[block, :], y_ref[...]) * in_bits
        s_ref[block, :] = s
        row_max = jnp.max(s, axis=1, keepdims=True)
        row_sum = jnp.sum(jnp.exp2(s - row_max), axis=1, keepdims=True)
        row_norm.append(row_max + (jnp.log2(row_sum) + shift))
        here_max = jnp.max(s, axis=0, keepdims=True)
        if i == 0:
            col_max = here_max
            col_sum = jnp.sum(jnp.exp2(s - col_max), axis=0, keepdims=True)
        else:
            new_max = jnp.maximum(col_max, here_max)
            col_sum = col_sum * jnp.exp2(col_max - new_max) + jnp.sum(
                jnp.exp2(s - new_max), axis=0, keepdims=True
            )
            col_max = new_max
    col_norm = col_max + (jnp.log2(col_sum) + shift)
    for i in range(chunks):
        block = pl.ds(i * CHUNK, CHUNK)
        s = s_ref[block, :]
        d = jnp.exp2(s - row_norm[i]) + jnp.exp2(s - col_norm)
        at = lax.broadcasted_iota(jnp.int32, d.shape, 0) + i * CHUNK
        d = jnp.where(at == lax.broadcasted_iota(jnp.int32, d.shape, 1), d - 2.0 * scale, d)
        emit(i, dot_nn(d.astype(BF16), y_ref[...]))


def round_kernel(
    rel_ref, rel_far_ref, e_ref, l_ref, r_ref, ops_ref, g_in_ref,
    e_out_ref, l_out_ref, g_ref, q_ref, q_far_ref, dq_ref, s_ref,
):
    rows = e_ref.shape[0]
    blocks = rel_ref.shape[0]
    size = rows // blocks
    for b in range(blocks):
        block = pl.ds(b * size, size)
        q_ref[block, :] = dot_nn(l_ref[block, :], ops_ref[rel_ref[b]]).astype(BF16)
        q_far_ref[block, :] = dot_nn(r_ref[block, :], ops_ref[rel_far_ref[b]]).astype(BF16)

    def own(i, value):
        dq_ref[pl.ds(i * CHUNK, CHUNK), :] = value.astype(BF16)

    two_way_gradient(q_ref, r_ref, s_ref, own)
    for b in range(blocks):
        block = pl.ds(b * size, size)
        e_out_ref[block, :] = dot_nt(dq_ref[block, :], ops_ref[rel_ref[b]])

    def far(i, value):
        block = pl.ds(i * CHUNK, CHUNK)
        moved = e_ref[block, :] - embed_rate * (e_out_ref[block, :] + value.astype(BF16).astype(F32))
        e_out_ref[block, :] = moved
        l_out_ref[block, :] = moved.astype(BF16)

    two_way_gradient(l_ref, q_far_ref, s_ref, far)
    g_ref[...] = g_in_ref[...]
    for b in range(blocks):
        block = pl.ds(b * size, size)
        g_ref[rel_ref[b]] += dot_tn(l_ref[block, :], dq_ref[block, :])


def run_round(rel, rel_far, e, left, right, ops, g):
    rows, width = e.shape
    vmem = pl.BlockSpec(memory_space=pltpu.VMEM)
    smem = pl.BlockSpec(memory_space=pltpu.SMEM)
    return pl.pallas_call(
        round_kernel,
        out_shape=(
            jax.ShapeDtypeStruct(e.shape, F32),
            jax.ShapeDtypeStruct(e.shape, BF16),
            jax.ShapeDtypeStruct(g.shape, F32),
        ),
        in_specs=[smem, smem] + [vmem] * 5,
        out_specs=(vmem,) * 3,
        input_output_aliases={6: 2},
        scratch_shapes=[
            pltpu.VMEM((rows, width), BF16),
            pltpu.VMEM((rows, width), BF16),
            pltpu.VMEM((rows, width), BF16),
            pltpu.VMEM((rows, rows), F32),
        ],
        compiler_params=pltpu.CompilerParams(vmem_limit_bytes=48 * 2**20),
    )(rel, rel_far, e, left, right, ops, g)


def fetch(left, rel, mask):
    count = lax.axis_size(AXES)

    def by(m):
        route = [(i, i ^ m) for i in range(count)]
        return lambda a, b: (lax.ppermute(a, AXES, route), lax.ppermute(b, AXES, route))

    return lax.switch(mask - 1, [by(m) for m in range(1, count)], left, rel)


def shards(embeddings, operators, plan, relations):
    ops = operators.astype(BF16)
    e = embeddings
    left = e.astype(BF16)
    g = jnp.zeros(operators.shape, F32)
    for r in range(ROUNDS):
        right, rel_far = fetch(left, relations[r], plan[r])
        e, left, g = run_round(relations[r], rel_far, e, left, right, ops, g)
    count = lax.axis_size(AXES)
    flat = g.astype(BF16).reshape(count, -1, operators.shape[2])
    parts = lax.all_to_all(flat, AXES, 0, 0, tiled=True)
    mine = jnp.sum(parts.astype(F32), axis=0, keepdims=True).astype(BF16)
    summed = lax.all_to_all(jnp.broadcast_to(mine, flat.shape), AXES, 0, 0, tiled=True)
    new_operators = operators - operator_rate * summed.astype(F32).reshape(operators.shape)
    return (e, new_operators)


def solution(mesh):
    return jax.shard_map(
        shards,
        mesh=mesh,
        in_specs=(P(AXES, None), P(), P(), P(None, AXES)),
        out_specs=(P(AXES, None), P()),
        check_vma=False,
    )
```

time: 537 us -> 355 us (0.66)
  waiting for transfers between devices: 311 us -> 28.5 us
  loops' own time: 1.02 us -> 130 us
  blocking collectives: 0 us -> 71.6 us
  matrix products: 57.7 us -> 0 us
  Pallas kernels: 0 us -> 51 us
  between operations: 33 us -> 3.77 us
  local copies, waits for them, and re-layouts: 40.1 us -> 11 us
  other arithmetic: 35.8 us -> 10 us
    ppermute x26 -> x8, waiting for transfers between devices: 252 us -> 28.5 us  [the longest x4 28.5 us: by(): lax.ppermute(b, AXES, route)]
    another operation x56 -> x4, loops' own time: 1.02 us -> 130 us  [fetch(): return lax.switch(mask - 1, [by(m) for m in range(1, count)], left, rel)]
    all_to_all x0 -> x2, blocking collectives: none -> 71.6 us  [the longest x1 37.1 us: shards(): parts = lax.all_to_all(flat, AXES, 0, 0, tiled=True)]
    psum x1 -> x0, waiting for transfers between devices: 59.1 us -> none  [shards(): summed = lax.psum(grad_total, ('group', 'member'))]
    dot_general x32 -> x0, matrix products: 57.7 us -> none  [the longest x4 9.88 us: shards(): jnp.dot(onehot.astype(jnp.float32).T, block_gradient, precision=lax.Preci...]
    pallas_call x0 -> x4, Pallas kernels: none -> 51 us  [run_round(): pl.pallas_call(round_kernel, out_shape=(jax.ShapeDtypeStruct(e.shape, F32...]
    cond x26 -> x0, local copies, waits for them, and re-layouts: 21.2 us -> none
    convert_element_type x9 -> x3, other arithmetic: 19.9 us -> 6.36 us  [the longest x1 2.64 us: shards(): ops = operators.astype(BF16)]
  transfers between devices with their start and end apart: 27 -> 8, of which waited for: 27 -> 4; matrix products, arithmetic and copies ran while one was open for 2% -> 0% of each run, Pallas kernels for 0% -> 0%
where the time goes in v1:
time: 355 us; the launch traced here: 351 us
  loops' own time  130 us (37%)
  blocking collectives  71.6 us (20%)
  Pallas kernels  51 us (14%)
  starting transfers between devices  45.4 us (13%)
  waiting for transfers between devices  28.5 us (8%)
  local copies, waits for them, and re-layouts  11 us (3%)
  other arithmetic  10 us (3%)
  between operations  3.77 us (1%)
    another operation x4, loops' own time, fetch(): return lax.switch(mask - 1, [by(m) for m in range(1, count)], left, rel)  130 us
    pallas_call x4, Pallas kernels, run_round(): pl.pallas_call(round_kernel, out_shape=(jax.ShapeDtypeStruct(e.shape, F32...  51 us
    all_to_all x1, blocking collectives, shards(): parts = lax.all_to_all(flat, AXES, 0, 0, tiled=True)  37.1 us
    all_to_all x1, blocking collectives, shards(): lax.all_to_all(jnp.broadcast_to(mine, flat.shape), AXES, 0, 0, tiled=True)  34.5 us
    ppermute x4, waiting for transfers between devices, by(): lax.ppermute(b, AXES, route)  28.5 us
    ppermute x4, starting transfers between devices, by(): lax.ppermute(b, AXES, route)  26.8 us
    ppermute x4, starting transfers between devices, by(): lax.ppermute(a, AXES, route)  18.6 us
  transfers between devices with their start and end apart: 8, of which 4 were waited for; matrix products, arithmetic and copies ran while one was open for 0% of the time, Pallas kernels for 0%

profile of v1, /device:TPU:1, one launch (start us, length us, event | category | flops | bytes accessed | tf_op | source)
XLA Modules:
  0.0 350.9 jit_solution(18216030996602071528)
XLA Ops:
  0.6 1.5 fusion
  4.7 0.8 slice_bitcast_fusion
  5.5 1.3 convert_element_type.19.l_ref
  6.8 0.0 copy-start.6
  6.8 0.0 copy-start
  6.8 2.6 convert_element_type.20.ops_ref
  9.5 0.0 copy-done.6
  9.5 39.6 %conditional.4 = (bf16[1024,256]{1,0:T(8,128)(2,1)}, s32[8]{0:T(128)}) conditional(s32[]{:T(128)} %bitcast.7, (bf16[1024,256]{1,0:T(8,128)(2,1)S(1)}, s32[8]{0:T(128)S(1)}) %tuple.2040, (bf16[1024,256]{1,0:T(8,128)(2,1)S(1)}, s32[8]{0:T(128)S(1)}) %tuple.2040, (bf16[1024,256]{1,0:T(8,128)(2,1)S(1)}, ...), branch_computations={%region_0.0_spmd, %region_1.0_spmd, %region_2.0_spmd, %region_3.0_... | conditional | bytes 2097376 | solution.py:132
  9.5 1.5 collective-permute-start
  11.0 0.1 collective-permute-start.1
  11.1 1.6 collective-permute-done.1
  12.7 0.0 collective-permute-done
  49.1 0.0 copy-start.7
  49.1 2.5 broadcast_in_dim.4.g_in_ref
  51.5 0.0 copy-done
  51.5 12.6 %shard_map.59 = (f32[1024,256]{1,0:T(8,128)S(1)}, bf16[1024,256]{1,0:T(8,128)(2,1)}, f32[16,256,256]{2,1,0:T(8,128)}) custom-call(s32[8]{0:T(128)S(1)} %get-tuple-element.3088.rel_ref, s32[8]{0:T(128)} %get-tuple-element.3069.rel_far_ref, f32[1024,256]{1,0:T(8,128)S(1)} %copy-done, bf16[1024,256]{1,0:T(8,128)(2,1)S(1)} %copy-done.7, ...), custom_call_target="tpu_custom_call", output_to_operand_aliasing={{2}: (6, {})} | custom-call | tf_op jit(solution)/shard_map/pallas_call | solution.py:105
  64.1 1.0 copy-done.3
  65.1 59.5 %conditional.5 = (bf16[1024,256]{1,0:T(8,128)(2,1)}, s32[8]{0:T(128)}) conditional(s32[]{:T(128)} %bitcast.5, (bf16[1024,256]{1,0:T(8,128)(2,1)}, s32[8]{0:T(128)S(1)}) %tuple.2041, (bf16[1024,256]{1,0:T(8,128)(2,1)}, s32[8]{0:T(128)S(1)}) %tuple.2041, (bf16[1024,256]{1,0:T(8,128)(2,1)}, s32[8]{0:T(128)S(1)}) %tuple.2041, ...), branch_computations={%region_127.0_spmd, %region_128.0_spmd, %region_129.0_spmd, %regio... | conditional | bytes 2097376 | solution.py:132
  75.2 9.7 %collective-permute-start.362 = (bf16[1024,256]{1,0:T(8,128)(2,1)}, bf16[1024,256]{1,0:T(8,128)(2,1)}, u32[]{:S(2)}, u32[]{:S(2)}) collective-permute-start(bf16[1024,256]{1,0:T(8,128)(2,1)} %get-tuple-element.2394), channel_id=1, source_target_pairs={{0,55},{1,54},{2,53},{3,52},{4,51},{5,50},{6,49},{7,48},{8,63},{9,... | collective-permute-start | bytes 1572872 | tf_op jit(solution)/shard_map/cond/branch_54_fun/ppermute | solution.py:130
  84.9 8.9 %collective-permute-start.363 = (s32[8]{0:T(128)S(1)}, s32[8]{0:T(128)}, u32[]{:S(2)}, u32[]{:S(2)}) collective-permute-start(s32[8]{0:T(128)S(1)} %get-tuple-element.2395), channel_id=1, source_target_pairs={{0,55},{1,54},{2,53},{3,52},{4,51},{5,50},{6,49},{7,48},{8,63},{9,... | collective-permute-start | bytes 104 | tf_op jit(solution)/shard_map/cond/branch_54_fun/ppermute | solution.py:130
  93.8 8.2 %collective-permute-done.363 = s32[8]{0:T(128)} collective-permute-done((s32[8]{0:T(128)S(1)}, s32[8]{0:T(128)}, u32[]{:S(2)}, u32[]{:S(2)}) %collective-permute-start.363) | collective-permute-done | bytes 64 | tf_op jit(solution)/shard_map/cond/branch_54_fun/ppermute | solution.py:130
  102.1 0.0 collective-permute-done.362
  124.6 0.0 copy-start.4
  124.6 1.2 copy-done.4
  125.9 12.8 %shard_map.60 = (f32[1024,256]{1,0:T(8,128)S(1)}, bf16[1024,256]{1,0:T(8,128)(2,1)}, f32[16,256,256]{2,1,0:T(8,128)}) custom-call(s32[8]{0:T(128)S(1)} %get-tuple-element.3091.rel_ref, s32[8]{0:T(128)} %get-tuple-element.3072.rel_far_ref, f32[1024,256]{1,0:T(8,128)S(1)} %copy-done.4, ...), custom_call_target="tpu_custom_call", output_to_operand_aliasing={{2}: (6, {})} | custom-call | tf_op jit(solution)/shard_map/pallas_call | solution.py:105
  138.6 1.0 copy-done.1
  139.6 54.0 %conditional.6 = (bf16[1024,256]{1,0:T(8,128)(2,1)}, s32[8]{0:T(128)}) conditional(s32[]{:T(128)} %bitcast.3, (bf16[1024,256]{1,0:T(8,128)(2,1)}, s32[8]{0:T(128)S(1)}) %tuple.2042, (bf16[1024,256]{1,0:T(8,128)(2,1)}, s32[8]{0:T(128)S(1)}) %tuple.2042, (bf16[1024,256]{1,0:T(8,128)(2,1)}, s32[8]{0:T(128)S(1)}) %tuple.2042, ...), branch_computations={%region_254.0_spmd, %region_255.0_spmd, %region_256.0_spmd, %regio... | conditional | bytes 2097376 | solution.py:132
  167.1 6.1 %collective-permute-start.760 = (bf16[1024,256]{1,0:T(8,128)(2,1)}, bf16[1024,256]{1,0:T(8,128)(2,1)}, u32[]{:S(2)}, u32[]{:S(2)}) collective-permute-start(bf16[1024,256]{1,0:T(8,128)(2,1)} %get-tuple-element.2792), channel_id=1, source_target_pairs={{0,127},{1,126},{2,125},{3,124},{4,123},{5,122},{6,121},{7,120},{8... | collective-permute-start | bytes 1572872 | tf_op jit(solution)/shard_map/cond/branch_126_fun/ppermute | solution.py:130
  173.2 8.9 %collective-permute-start.761 = (s32[8]{0:T(128)S(1)}, s32[8]{0:T(128)}, u32[]{:S(2)}, u32[]{:S(2)}) collective-permute-start(s32[8]{0:T(128)S(1)} %get-tuple-element.2793), channel_id=1, source_target_pairs={{0,127},{1,126},{2,125},{3,124},{4,123},{5,122},{6,121},{7,120},{8... | collective-permute-start | bytes 104 | tf_op jit(solution)/shard_map/cond/branch_126_fun/ppermute | solution.py:130
  182.1 11.3 %collective-permute-done.761 = s32[8]{0:T(128)} collective-permute-done((s32[8]{0:T(128)S(1)}, s32[8]{0:T(128)}, u32[]{:S(2)}, u32[]{:S(2)}) %collective-permute-start.761) | collective-permute-done | bytes 64 | tf_op jit(solution)/shard_map/cond/branch_126_fun/ppermute | solution.py:130
  193.4 0.0 collective-permute-done.760
  193.7 0.0 copy-start.2
  193.7 1.2 copy-done.2
  194.9 12.8 %shard_map.61 = (f32[1024,256]{1,0:T(8,128)S(1)}, bf16[1024,256]{1,0:T(8,128)(2,1)}, f32[16,256,256]{2,1,0:T(8,128)}) custom-call(s32[8]{0:T(128)S(1)} %get-tuple-element.3089.rel_ref, s32[8]{0:T(128)} %get-tuple-element.3077.rel_far_ref, f32[1024,256]{1,0:T(8,128)S(1)} %copy-done.2, ...), custom_call_target="tpu_custom_call", output_to_operand_aliasing={{2}: (6, {})} | custom-call | tf_op jit(solution)/shard_map/pallas_call | solution.py:105
  207.7 50.5 %conditional.7 = (bf16[1024,256]{1,0:T(8,128)(2,1)}, s32[8]{0:T(128)}) conditional(s32[]{:T(128)} %bitcast.1, (bf16[1024,256]{1,0:T(8,128)(2,1)}, s32[8]{0:T(128)S(1)}) %tuple.2043, (bf16[1024,256]{1,0:T(8,128)(2,1)}, s32[8]{0:T(128)S(1)}) %tuple.2043, (bf16[1024,256]{1,0:T(8,128)(2,1)}, s32[8]{0:T(128)S(1)}) %tuple.2043, ...), branch_computations={%region_381.0_spmd, %region_382.0_spmd, %region_383.0_spmd, %regio... | conditional | bytes 2097376 | solution.py:132
  214.8 1.3 collective-permute-start.806
  216.1 8.9 %collective-permute-start.807 = (s32[8]{0:T(128)S(1)}, s32[8]{0:T(128)}, u32[]{:S(2)}, u32[]{:S(2)}) collective-permute-start(s32[8]{0:T(128)S(1)} %get-tuple-element.2839), channel_id=1, source_target_pairs={{0,23},{1,22},{2,21},{3,20},{4,19},{5,18},{6,17},{7,16},{8,31},{9,... | collective-permute-start | bytes 104 | tf_op jit(solution)/shard_map/cond/branch_22_fun/ppermute | solution.py:130
  225.0 7.3 %collective-permute-done.807 = s32[8]{0:T(128)} collective-permute-done((s32[8]{0:T(128)S(1)}, s32[8]{0:T(128)}, u32[]{:S(2)}, u32[]{:S(2)}) %collective-permute-start.807) | collective-permute-done | bytes 64 | tf_op jit(solution)/shard_map/cond/branch_22_fun/ppermute | solution.py:130
  232.4 0.0 collective-permute-done.806
  258.1 12.8 %shard_map.62 = (f32[1024,256]{1,0:T(8,128)}, bf16[1024,256]{1,0:T(8,128)(2,1)}, f32[16,256,256]{2,1,0:T(8,128)}) custom-call(s32[8]{0:T(128)S(1)} %get-tuple-element.3090.rel_ref, s32[8]{0:T(128)} %get-tuple-element.3082.rel_far_ref, f32[1024,256]{1,0:T(8,128)S(1)} %get-tuple-element.3083.e_ref, ...), custom_call_target="tpu_custom_call", output_to_operand_aliasing={{2}: (6, {})} | custom-call | tf_op jit(solution)/shard_map/pallas_call | solution.py:105
  270.9 2.4 convert_element_type.21
  273.4 37.1 %all_to_all.10 = bf16[128,32,256]{2,1,0:T(8,128)(2,1)S(1)} all-to-all(bf16[128,32,256]{2,1,0:T(8,128)(2,1)S(1)} %bitcast.17), channel_id=1, replica_groups=mesh['group'=8,'member'=16] {'group','member'}, dimensions={0} | all-to-all | bytes 4194304 | tf_op jit(solution)/shard_map/all_to_all | solution.py:145
  310.5 0.3 reduce_sum.12
  310.8 0.3 broadcast_in_dim.10
  311.1 34.5 %all_to_all.11 = bf16[128,32,256]{2,1,0:T(8,128)(2,1)S(1)} all-to-all(bf16[128,32,256]{2,1,0:T(8,128)(2,1)S(1)} %broadcast_in_dim.10), channel_id=1, replica_groups=mesh['group'=8,'member'=16] {'group','member'}, dimensions={0} | all-to-all | bytes 4194304 | tf_op jit(solution)/shard_map/all_to_all | solution.py:147
  345.6 0.6 convert_multiply_fusion
  346.2 1.6 copy-done.5
  347.8 2.7 bitcast_subtract_fusion
  (4 shorter events, 0.0 us)
Async XLA Ops:
  6.8 2.7 copy-start.6
  6.8 44.7 %copy-start = (f32[1024,256]{1,0:T(8,128)S(1)}, f32[1024,256]{1,0:T(8,128)}, u32[]{:S(2)}) copy-start(f32[1024,256]{1,0:T(8,128)} %e_ref.1) | copy-start | bytes 3145732
  9.5 3.2 collective-permute-start
  11.0 1.7 collective-permute-start.1
  49.1 2.5 copy-start.7
  64.1 1.0 copy-start.3
  75.2 26.8 %collective-permute-start.362 = (bf16[1024,256]{1,0:T(8,128)(2,1)}, bf16[1024,256]{1,0:T(8,128)(2,1)}, u32[]{:S(2)}, u32[]{:S(2)}) collective-permute-start(bf16[1024,256]{1,0:T(8,128)(2,1)} %get-tuple-element.2394), channel_id=1, source_target_pairs={{0,55},{1,54},{2,53},{3,52},{4,51},{5,50},{6,49},{7,48},{8,63},{9,... | collective-permute-start | bytes 1572872 | tf_op jit(solution)/shard_map/cond/branch_54_fun/ppermute | solution.py:130
  84.9 17.1 %collective-permute-start.363 = (s32[8]{0:T(128)S(1)}, s32[8]{0:T(128)}, u32[]{:S(2)}, u32[]{:S(2)}) collective-permute-start(s32[8]{0:T(128)S(1)} %get-tuple-element.2395), channel_id=1, source_target_pairs={{0,55},{1,54},{2,53},{3,52},{4,51},{5,50},{6,49},{7,48},{8,63},{9,... | collective-permute-start | bytes 104 | tf_op jit(solution)/shard_map/cond/branch_54_fun/ppermute | solution.py:130
  124.6 1.2 copy-start.4
  138.6 1.0 copy-start.1
  167.1 26.3 %collective-permute-start.760 = (bf16[1024,256]{1,0:T(8,128)(2,1)}, bf16[1024,256]{1,0:T(8,128)(2,1)}, u32[]{:S(2)}, u32[]{:S(2)}) collective-permute-start(bf16[1024,256]{1,0:T(8,128)(2,1)} %get-tuple-element.2792), channel_id=1, source_target_pairs={{0,127},{1,126},{2,125},{3,124},{4,123},{5,122},{6,121},{7,120},{8... | collective-permute-start | bytes 1572872 | tf_op jit(solution)/shard_map/cond/branch_126_fun/ppermute | solution.py:130
  173.2 20.2 %collective-permute-start.761 = (s32[8]{0:T(128)S(1)}, s32[8]{0:T(128)}, u32[]{:S(2)}, u32[]{:S(2)}) collective-permute-start(s32[8]{0:T(128)S(1)} %get-tuple-element.2793), channel_id=1, source_target_pairs={{0,127},{1,126},{2,125},{3,124},{4,123},{5,122},{6,121},{7,120},{8... | collective-permute-start | bytes 104 | tf_op jit(solution)/shard_map/cond/branch_126_fun/ppermute | solution.py:130
  193.7 1.2 copy-start.2
  214.8 17.6 %collective-permute-start.806 = (bf16[1024,256]{1,0:T(8,128)(2,1)}, bf16[1024,256]{1,0:T(8,128)(2,1)}, u32[]{:S(2)}, u32[]{:S(2)}) collective-permute-start(bf16[1024,256]{1,0:T(8,128)(2,1)} %get-tuple-element.2838), channel_id=1, source_target_pairs={{0,23},{1,22},{2,21},{3,20},{4,19},{5,18},{6,17},{7,16},{8,31},{9,... | collective-permute-start | bytes 1572872 | tf_op jit(solution)/shard_map/cond/branch_22_fun/ppermute | solution.py:130
  216.1 16.2 %collective-permute-start.807 = (s32[8]{0:T(128)S(1)}, s32[8]{0:T(128)}, u32[]{:S(2)}, u32[]{:S(2)}) collective-permute-start(s32[8]{0:T(128)S(1)} %get-tuple-element.2839), channel_id=1, source_target_pairs={{0,23},{1,22},{2,21},{3,20},{4,19},{5,18},{6,17},{7,16},{8,31},{9,... | collective-permute-start | bytes 104 | tf_op jit(solution)/shard_map/cond/branch_22_fun/ppermute | solution.py:130
  345.6 2.2 copy-start.5

commit v2 on v1

v2 whole, which is shorter than its diff:
```python
import functools
import math

import jax
import jax.numpy as jnp
from jax import lax
from jax.experimental import pallas as pl
from jax.experimental.pallas import tpu as pltpu
from jax.sharding import PartitionSpec as P

ROUNDS = 4
AXES = ("chip", "core")
ID_ROWS = 16
CHUNK = 256
F32 = jnp.float32
BF16 = jnp.bfloat16

embed_rate = 1.0
operator_rate = 0.02


def dot_nt(a, b):
    return lax.dot_general(a, b, (((1,), (1,)), ((), ())), preferred_element_type=F32)


def dot_nn(a, b):
    return lax.dot_general(a, b, (((1,), (0,)), ((), ())), preferred_element_type=F32)


def dot_tn(a, b):
    return lax.dot_general(a, b, (((0,), (0,)), ((), ())), preferred_element_type=F32)


def two_way_gradient(x_ref, y_ref, s_ref, rows, emit):
    width = x_ref.shape[1]
    every = pl.ds(0, rows)
    chunks = rows // CHUNK
    scale = 1.0 / math.sqrt(width)
    in_bits = scale * math.log2(math.e)
    shift = -math.log2(scale)
    row_norm = []
    col_max = col_sum = None
    for i in range(chunks):
        block = pl.ds(i * CHUNK, CHUNK)
        s = dot_nt(x_ref[block, :], y_ref[every, :]) * in_bits
        s_ref[block, :] = s
        row_max = jnp.max(s, axis=1, keepdims=True)
        row_sum = jnp.sum(jnp.exp2(s - row_max), axis=1, keepdims=True)
        row_norm.append(row_max + (jnp.log2(row_sum) + shift))
        here_max = jnp.max(s, axis=0, keepdims=True)
        if i == 0:
            col_max = here_max
            col_sum = jnp.sum(jnp.exp2(s - col_max), axis=0, keepdims=True)
        else:
            new_max = jnp.maximum(col_max, here_max)
            col_sum = col_sum * jnp.exp2(col_max - new_max) + jnp.sum(
                jnp.exp2(s - new_max), axis=0, keepdims=True
            )
            col_max = new_max
    col_norm = col_max + (jnp.log2(col_sum) + shift)
    for i in range(chunks):
        block = pl.ds(i * CHUNK, CHUNK)
        s = s_ref[block, :]
        d = jnp.exp2(s - row_norm[i]) + jnp.exp2(s - col_norm)
        at = lax.broadcasted_iota(jnp.int32, d.shape, 0) + i * CHUNK
        d = jnp.where(at == lax.broadcasted_iota(jnp.int32, d.shape, 1), d - 2.0 * scale, d)
        emit(i, dot_nn(d.astype(BF16), y_ref[every, :]))


def write_payload(out_ref, value, block):
    out_ref[block, :] = value.astype(BF16)


def write_ids(out_ref, rel_ref):
    rows = out_ref.shape[0] - ID_ROWS
    lane = lax.broadcasted_iota(jnp.int32, (ID_ROWS, out_ref.shape[1]), 1)
    ids = jnp.zeros(lane.shape, jnp.int32)
    for b in range(rel_ref.shape[0]):
        ids = jnp.where(lane == b, rel_ref[b], ids)
    out_ref[pl.ds(rows, ID_ROWS), :] = ids.astype(F32).astype(BF16)


def read_ids(payload_ref, count):
    rows = payload_ref.shape[0] - ID_ROWS
    ids = payload_ref[pl.ds(rows, ID_ROWS), :].astype(F32)
    lane = lax.broadcasted_iota(jnp.int32, ids.shape, 1)
    return [jnp.max(jnp.where(lane == b, ids, 0.0)).astype(jnp.int32) for b in range(count)]


def prepare_kernel(rel_ref, e_ref, out_ref):
    write_payload(out_ref, e_ref[...], pl.ds(0, e_ref.shape[0]))
    write_ids(out_ref, rel_ref)


def round_kernel(first, last, *refs):
    refs = list(refs)
    rel_ref = refs.pop(0)
    next_ref = None if last else refs.pop(0)
    e_ref, l_ref, r_ref, table_ref = refs[:4]
    refs = refs[4:]
    history = [refs.pop(0) for _ in range(3 * (ROUNDS - 1))] if last else None
    e_out_ref = refs.pop(0)
    if last:
        g_out_ref = refs.pop(0)
    else:
        l_out_ref, dq_ref = refs[:2]
        refs = refs[2:]
    ops_ref = refs.pop(0) if first else table_ref
    q_ref, q_far_ref, s_ref = refs[:3]
    if last:
        dq_ref, g_ref = refs[3:]
    rows = e_ref.shape[0]
    blocks = rel_ref.shape[0]
    size = rows // blocks
    if first:
        ops_ref[...] = table_ref[...].astype(BF16)
    rel_far = read_ids(r_ref, blocks)
    for b in range(blocks):
        block = pl.ds(b * size, size)
        q_ref[block, :] = dot_nn(l_ref[block, :], ops_ref[rel_ref[b]]).astype(BF16)
        q_far_ref[block, :] = dot_nn(r_ref[block, :], ops_ref[rel_far[b]]).astype(BF16)

    def own(i, value):
        dq_ref[pl.ds(i * CHUNK, CHUNK), :] = value.astype(BF16)

    two_way_gradient(q_ref, r_ref, s_ref, rows, own)
    for b in range(blocks):
        block = pl.ds(b * size, size)
        e_out_ref[block, :] = dot_nt(dq_ref[block, :], ops_ref[rel_ref[b]])

    def far(i, value):
        block = pl.ds(i * CHUNK, CHUNK)
        moved = e_ref[block, :] - embed_rate * (e_out_ref[block, :] + value.astype(BF16).astype(F32))
        e_out_ref[block, :] = moved
        if not last:
            write_payload(l_out_ref, moved, block)

    two_way_gradient(l_ref, q_far_ref, s_ref, rows, far)
    if not last:
        write_ids(l_out_ref, next_ref)
        return
    g_ref[...] = jnp.zeros(g_ref.shape, F32)
    for ids, left, grad in [history[k : k + 3] for k in range(0, len(history), 3)] + [
        (rel_ref, l_ref, dq_ref)
    ]:
        for b in range(blocks):
            block = pl.ds(b * size, size)
            g_ref[ids[b]] += dot_tn(left[block, :], grad[block, :])
    g_out_ref[...] = g_ref[...].astype(BF16)


def run_round(index, relations, e, left, right, table, history):
    first, last = index == 0, index == ROUNDS - 1
    rows, width = e.shape
    vmem = pl.BlockSpec(memory_space=pltpu.VMEM)
    smem = pl.BlockSpec(memory_space=pltpu.SMEM)
    args = [relations[index]] + ([] if last else [relations[index + 1]])
    specs = [smem] * len(args)
    args += [e, left, right, table]
    specs += [vmem] * 4
    shapes = [jax.ShapeDtypeStruct(e.shape, F32)]
    scratch = [pltpu.VMEM((rows, width), BF16)] * 2 + [pltpu.VMEM((rows, rows), F32)]
    if last:
        for k, (old_left, old_grad) in enumerate(history):
            args += [relations[k], old_left, old_grad]
            specs += [smem, vmem, vmem]
        shapes.append(jax.ShapeDtypeStruct(table.shape, BF16))
        scratch += [pltpu.VMEM((rows, width), BF16), pltpu.VMEM(table.shape, F32)]
    else:
        shapes += [jax.ShapeDtypeStruct(left.shape, BF16), jax.ShapeDtypeStruct(e.shape, BF16)]
    if first:
        shapes.append(jax.ShapeDtypeStruct(table.shape, BF16))
    return pl.pallas_call(
        functools.partial(round_kernel, first, last),
        out_shape=tuple(shapes),
        in_specs=specs,
        out_specs=(vmem,) * len(shapes),
        scratch_shapes=scratch,
        compiler_params=pltpu.CompilerParams(vmem_limit_bytes=44 * 2**20),
    )(*args)


def prepare(rel, e):
    rows, width = e.shape
    return pl.pallas_call(
        prepare_kernel,
        out_shape=jax.ShapeDtypeStruct((rows + ID_ROWS, width), BF16),
        in_specs=[pl.BlockSpec(memory_space=pltpu.SMEM), pl.BlockSpec(memory_space=pltpu.VMEM)],
        out_specs=pl.BlockSpec(memory_space=pltpu.VMEM),
    )(rel, e)


def fetch(values, mask):
    count = lax.axis_size(AXES)

    def pick(known, bit):
        if bit == 0:
            route = [(i, i ^ known) for i in range(count)]
            return lambda x: lax.ppermute(x, AXES, route)
        half = 1 << (bit - 1)
        high, low = pick(known | half, bit - 1), pick(known, bit - 1)
        return lambda x: lax.cond((mask & half) != 0, high, low, x)

    return pick(0, count.bit_length() - 1)(values)


def reduce_operators(g):
    slots = g.shape[0]
    width = g.shape[2]
    chips = lax.axis_size("chip")
    core = lax.axis_index("core")
    halves = g.reshape(2, slots // 2, width, width)
    kept = lax.dynamic_index_in_dim(halves, core, 0, keepdims=False)
    given = lax.dynamic_index_in_dim(halves, 1 - core, 0, keepdims=False)
    swap = [(0, 1), (1, 0)]
    pair = (kept.astype(F32) + lax.ppermute(given, "core", swap).astype(F32)).astype(BF16)
    parts = lax.all_to_all(pair.reshape(chips, -1, width), "chip", 0, 0, tiled=True)
    mine = jnp.sum(parts.astype(F32), axis=0, keepdims=True).astype(BF16)
    half = lax.all_to_all(jnp.broadcast_to(mine, parts.shape), "chip", 0, 0, tiled=True)
    half = half.reshape(slots // 2, width, width)
    other = lax.ppermute(half, "core", swap)
    return jnp.concatenate([jnp.where(core == 0, half, other), jnp.where(core == 0, other, half)])


def shards(embeddings, operators, plan, relations):
    e, table, history = embeddings, operators, []
    left = prepare(relations[0], e)
    for r in range(ROUNDS):
        right = fetch(left, plan[r])
        out = run_round(r, relations, e, left, right, table, history)
        if r == ROUNDS - 1:
            e, g = out
            break
        history.append((left, out[2]))
        e, left = out[:2]
        if r == 0:
            table = out[3]
    return (e, operators - operator_rate * reduce_operators(g).astype(F32))


def solution(mesh):
    pairs = jax.sharding.Mesh(mesh.devices.reshape(-1, 2), AXES)
    return jax.shard_map(
        shards,
        mesh=pairs,
        in_specs=(P(AXES, None), P(), P(), P(None, AXES)),
        out_specs=(P(AXES, None), P()),
        check_vma=False,
    )
```

time: 355 us -> 306 us (0.86)
  waiting for transfers between devices: 28.5 us -> 60.1 us
  blocking collectives: 71.6 us -> 44 us
  starting transfers between devices: 45.4 us -> 18.8 us
  loops' own time: 130 us -> 109 us
  Pallas kernels: 51 us -> 42.8 us
  local copies, waits for them, and re-layouts: 11 us -> 17.2 us
  other arithmetic: 10 us -> 4.34 us
    ppermute x8 -> x6, waiting for transfers between devices: 28.5 us -> 60.1 us  [the longest x4 55.4 us: pick(): return lambda x: lax.ppermute(x, AXES, route)]
    all_to_all x2, blocking collectives: 71.6 us -> 44 us  [the longest x1 23.1 us: reduce_operators(): lax.all_to_all(jnp.broadcast_to(mine, parts.shape), 'chip', 0, 0, tiled=T...]
    ppermute x8 -> x6, starting transfers between devices: 45.4 us -> 18.8 us  [the longest x4 17 us: pick(): return lambda x: lax.ppermute(x, AXES, route)]
    another operation x4 -> x28, loops' own time: 130 us -> 109 us  [pick(): return lambda x: lax.cond(mask & half != 0, high, low, x)]
    unnamed x16 -> x30, local copies, waits for them, and re-layouts: 5.97 us -> 14.2 us
    pallas_call x4 -> x5, Pallas kernels: 51 us -> 42.8 us  [the longest x4 40.7 us: run_round(): pl.pallas_call(functools.partial(round_kernel, first, last), out_shape=tu...]
    convert_element_type x3 -> x1, other arithmetic: 6.36 us -> 1.47 us  [reduce_operators(): (kept.astype(F32) + lax.ppermute(given, 'core', swap).astype(F32)).astype...]
  transfers between devices with their start and end apart: 8 -> 6, of which waited for: 4 -> 6; matrix products, arithmetic and copies ran while one was open for 0% -> 0% of each run, Pallas kernels for 0% -> 0%
where the time goes in v2:
time: 306 us; the launch traced here: 301 us
  loops' own time  109 us (36%)
  waiting for transfers between devices  60.1 us (20%)
  blocking collectives  44 us (14%)
  Pallas kernels  42.8 us (14%)
  starting transfers between devices  18.8 us (6%)
  local copies, waits for them, and re-layouts  17.2 us (6%)
  other arithmetic  4.34 us (1%)
  between operations  3.88 us (1%)
    another operation x28, loops' own time, pick(): return lambda x: lax.cond(mask & half != 0, high, low, x)  109 us
    ppermute x4, waiting for transfers between devices, pick(): return lambda x: lax.ppermute(x, AXES, route)  55.4 us
    pallas_call x4, Pallas kernels, run_round(): pl.pallas_call(functools.partial(round_kernel, first, last), out_shape=tu...  40.7 us
    all_to_all x1, blocking collectives, reduce_operators(): lax.all_to_all(jnp.broadcast_to(mine, parts.shape), 'chip', 0, 0, tiled=T...  23.1 us
    all_to_all x1, blocking collectives, reduce_operators(): lax.all_to_all(pair.reshape(chips, -1, width), 'chip', 0, 0, tiled=True)  21 us
    ppermute x4, starting transfers between devices, pick(): return lambda x: lax.ppermute(x, AXES, route)  17 us
    unnamed x30, local copies, waits for them, and re-layouts  14.2 us
  transfers between devices with their start and end apart: 6, of which 6 were waited for; matrix products, arithmetic and copies ran while one was open for 0% of the time, Pallas kernels for 0%

profile of v2, /device:TPU:1, one launch (start us, length us, event | category | flops | bytes accessed | tf_op | source)
XLA Modules:
  0.0 300.6 jit_solution(4123040343460565234)
XLA Ops:
  2.0 1.5 fusion.1
  3.5 2.1 shard_map.59.refs_3_.refs_6_
  6.8 43.1 %conditional.508 = (bf16[1040,256]{1,0:T(8,128)(2,1)}) conditional(s32[]{:T(128)} %convert_element_type.1546, (s32[]{:T(128)}, bf16[1040,256]{1,0:T(8,128)(2,1)}) %tuple.2560, (s32[]{:T(128)}, bf16[1040,256]{1,0:T(8,128)(2,1)}) %tuple.2560), branch_computations={%region_0.0_spmd, %region_127.0_spmd} | conditional | flops 18 | bytes 2130124 | solution.py:202
  7.5 22.8 %conditional.62 = (bf16[1040,256]{1,0:T(8,128)(2,1)}) conditional(s32[]{:T(128)} %convert_element_type.1095, (s32[]{:T(128)}, bf16[1040,256]{1,0:T(8,128)(2,1)}) %param.126, (s32[]{:T(128)}, bf16[1040,256]{1,0:T(8,128)(2,1)}) %param.126), branch_computations={%region_1.0_spmd, %region_64.0_spmd} | conditional | flops 15 | bytes 2130098 | solution.py:202
  8.1 21.0 %conditional.30 = (bf16[1040,256]{1,0:T(8,128)(2,1)}) conditional(s32[]{:T(128)} %convert_element_type.1063, (s32[]{:T(128)}, bf16[1040,256]{1,0:T(8,128)(2,1)}) %param.62, (s32[]{:T(128)}, bf16[1040,256]{1,0:T(8,128)(2,1)}) %param.62), branch_computations={%region_2.0_spmd, %region_33.0_spmd} | conditional | flops 12 | bytes 2130072 | solution.py:202
  8.8 20.3 %conditional.14 = (bf16[1040,256]{1,0:T(8,128)(2,1)}) conditional(s32[]{:T(128)} %convert_element_type.1047, (s32[]{:T(128)}, bf16[1040,256]{1,0:T(8,128)(2,1)}) %param.30, (s32[]{:T(128)}, bf16[1040,256]{1,0:T(8,128)(2,1)}) %param.30), branch_computations={%region_3.0_spmd, %region_18.0_spmd} | conditional | flops 9 | bytes 2130046 | solution.py:202
  9.4 19.7 %conditional.13 = (bf16[1040,256]{1,0:T(8,128)(2,1)}) conditional(s32[]{:T(128)} %convert_element_type.1046, (s32[]{:T(128)}, bf16[1040,256]{1,0:T(8,128)(2,1)}) %param.29, (s32[]{:T(128)}, bf16[1040,256]{1,0:T(8,128)(2,1)}) %param.29), branch_computations={%region_19.0_spmd, %region_26.0_spmd} | conditional | flops 6 | bytes 2130020 | solution.py:202
  10.1 19.0 %conditional.12 = (bf16[1040,256]{1,0:T(8,128)(2,1)}) conditional(s32[]{:T(128)} %convert_element_type.1045, (s32[]{:T(128)}, bf16[1040,256]{1,0:T(8,128)(2,1)}) %param.28, (s32[]{:T(128)}, bf16[1040,256]{1,0:T(8,128)(2,1)}) %param.28), branch_computations={%region_27.0_spmd, %region_30.0_spmd} | conditional | flops 3 | bytes 2129994 | solution.py:202
  10.7 18.4 %conditional.11 = (bf16[1040,256]{1,0:T(8,128)(2,1)}) conditional(s32[]{:T(128)} %convert_element_type.1044, bf16[1040,256]{1,0:T(8,128)(2,1)} %get-tuple-element.4071, bf16[1040,256]{1,0:T(8,128)(2,1)} %get-tuple-element.4071), branch_computations={%region_31.0_spmd, %region_32.0_spmd} | conditional | bytes 2129968 | solution.py:202
  10.7 6.2 %collective-permute-start.15 = (bf16[1040,256]{1,0:T(8,128)(2,1)}, bf16[1040,256]{1,0:T(8,128)(2,1)}, u32[]{:S(2)}, u32[]{:S(2)}) collective-permute-start(bf16[1040,256]{1,0:T(8,128)(2,1)} %param.26), channel_id=1, source_target_pairs={{0,15},{1,14},{2,13},{3,12},{4,11},{5,10},{6,9},{7,8},{8,7},{9,6},... | collective-permute-start | bytes 1597448 | tf_op jit(solution)/shard_map/cond/branch_0_fun/cond/branch_0_fun/cond/branch_0_fun/cond/branch_1_fun/cond/branch_1_fun/cond/branch_1_fun/cond/branch_1_fun/ppermute | solution.py:199
  16.9 12.2 %collective-permute-done.15 = bf16[1040,256]{1,0:T(8,128)(2,1)} collective-permute-done((bf16[1040,256]{1,0:T(8,128)(2,1)}, bf16[1040,256]{1,0:T(8,128)(2,1)}, u32[]{:S(2)}, u32[]{:S(2)}) %collective-permute-start.15) | collective-permute-done | bytes 532512 | tf_op jit(solution)/shard_map/cond/branch_0_fun/cond/branch_0_fun/cond/branch_0_fun/cond/branch_1_fun/cond/branch_1_fun/cond/branch_1_fun/cond/branch_1_fun/ppermute | solution.py:199
  50.0 2.2 copy-done
  52.2 9.9 %shard_map.60 = (f32[1024,256]{1,0:T(8,128)S(1)}, bf16[1040,256]{1,0:T(8,128)(2,1)}, bf16[1024,256]{1,0:T(8,128)(2,1)S(1)}, bf16[16,256,256]{2,1,0:T(8,128)(2,1)S(1)}) custom-call(s32[8]{0:T(128)S(1)} %copy-done.14, s32[8]{0:T(128)S(1)} %get-tuple-element.4843.refs_1_.refs_0_.refs_8_, f32[1024,256]{1,0:T(8,128)S(1)} %copy-done.2, ...), custom_call_target="tpu_custom_call" | custom-call | tf_op jit(solution)/shard_map/pallas_call | solution.py:173
  64.5 56.7 %conditional.509 = (bf16[1040,256]{1,0:T(8,128)(2,1)}) conditional(s32[]{:T(128)} %convert_element_type.1547, (s32[]{:T(128)}, bf16[1040,256]{1,0:T(8,128)(2,1)}) %tuple.2561, (s32[]{:T(128)}, bf16[1040,256]{1,0:T(8,128)(2,1)}) %tuple.2561), branch_computations={%region_254.0_spmd, %region_381.0_spmd} | conditional | flops 18 | bytes 2130124 | solution.py:202
  74.1 38.2 %conditional.251 = (bf16[1040,256]{1,0:T(8,128)(2,1)}) conditional(s32[]{:T(128)} %convert_element_type.1284, (s32[]{:T(128)}, bf16[1040,256]{1,0:T(8,128)(2,1)}) %param.507, (s32[]{:T(128)}, bf16[1040,256]{1,0:T(8,128)(2,1)}) %param.507), branch_computations={%region_382.0_spmd, %region_445.0_spmd} | conditional | flops 15 | bytes 2130098 | solution.py:202
  74.7 37.3 %conditional.250 = (bf16[1040,256]{1,0:T(8,128)(2,1)}) conditional(s32[]{:T(128)} %convert_element_type.1283, (s32[]{:T(128)}, bf16[1040,256]{1,0:T(8,128)(2,1)}) %param.506, (s32[]{:T(128)}, bf16[1040,256]{1,0:T(8,128)(2,1)}) %param.506), branch_computations={%region_446.0_spmd, %region_477.0_spmd} | conditional | flops 12 | bytes 2130072 | solution.py:202
  80.5 31.6 %conditional.249 = (bf16[1040,256]{1,0:T(8,128)(2,1)}) conditional(s32[]{:T(128)} %convert_element_type.1282, (s32[]{:T(128)}, bf16[1040,256]{1,0:T(8,128)(2,1)}) %param.505, (s32[]{:T(128)}, bf16[1040,256]{1,0:T(8,128)(2,1)}) %param.505), branch_computations={%region_478.0_spmd, %region_493.0_spmd} | conditional | flops 9 | bytes 2130046 | solution.py:202
  81.1 31.0 %conditional.248 = (bf16[1040,256]{1,0:T(8,128)(2,1)}) conditional(s32[]{:T(128)} %convert_element_type.1281, (s32[]{:T(128)}, bf16[1040,256]{1,0:T(8,128)(2,1)}) %param.504, (s32[]{:T(128)}, bf16[1040,256]{1,0:T(8,128)(2,1)}) %param.504), branch_computations={%region_494.0_spmd, %region_501.0_spmd} | conditional | flops 6 | bytes 2130020 | solution.py:202
  81.8 30.3 %conditional.247 = (bf16[1040,256]{1,0:T(8,128)(2,1)}) conditional(s32[]{:T(128)} %convert_element_type.1280, (s32[]{:T(128)}, bf16[1040,256]{1,0:T(8,128)(2,1)}) %param.503, (s32[]{:T(128)}, bf16[1040,256]{1,0:T(8,128)(2,1)}) %param.503), branch_computations={%region_502.0_spmd, %region_505.0_spmd} | conditional | flops 3 | bytes 2129994 | solution.py:202
  82.4 29.6 %conditional.246 = (bf16[1040,256]{1,0:T(8,128)(2,1)}) conditional(s32[]{:T(128)} %convert_element_type.1279, bf16[1040,256]{1,0:T(8,128)(2,1)} %get-tuple-element.4426, bf16[1040,256]{1,0:T(8,128)(2,1)} %get-tuple-element.4426), branch_computations={%region_506.0_spmd, %region_507.0_spmd} | conditional | bytes 2129968 | solution.py:202
  82.4 9.2 %collective-permute-start.255 = (bf16[1040,256]{1,0:T(8,128)(2,1)}, bf16[1040,256]{1,0:T(8,128)(2,1)}, u32[]{:S(2)}, u32[]{:S(2)}) collective-permute-start(bf16[1040,256]{1,0:T(8,128)(2,1)} %param.501), channel_id=1, source_target_pairs={{0,127},{1,126},{2,125},{3,124},{4,123},{5,122},{6,121},{7,120},{8... | collective-permute-start | bytes 1597448 | tf_op jit(solution)/shard_map/cond/branch_1_fun/cond/branch_1_fun/cond/branch_1_fun/cond/branch_1_fun/cond/branch_1_fun/cond/branch_1_fun/cond/branch_1_fun/ppermute | solution.py:199
  91.7 20.4 %collective-permute-done.255 = bf16[1040,256]{1,0:T(8,128)(2,1)} collective-permute-done((bf16[1040,256]{1,0:T(8,128)(2,1)}, bf16[1040,256]{1,0:T(8,128)(2,1)}, u32[]{:S(2)}, u32[]{:S(2)}) %collective-permute-start.255) | collective-permute-done | bytes 532512 | tf_op jit(solution)/shard_map/cond/branch_1_fun/cond/branch_1_fun/cond/branch_1_fun/cond/branch_1_fun/cond/branch_1_fun/cond/branch_1_fun/cond/branch_1_fun/ppermute | solution.py:199
  121.2 9.6 %shard_map.61 = (f32[1024,256]{1,0:T(8,128)S(1)}, bf16[1040,256]{1,0:T(8,128)(2,1)}, bf16[1024,256]{1,0:T(8,128)(2,1)S(1)}) custom-call(s32[8]{0:T(128)S(1)} %get-tuple-element.4843.refs_1_.refs_0_.refs_8_, s32[8]{0:T(128)S(1)} %get-tuple-element.4841.refs_1_.refs_0_.refs_11_, f32[1024,256]{1,0:T(8,128)S(1)} %copy-done.7, ...), custom_call_target="tpu_custom_call" | custom-call | tf_op jit(solution)/shard_map/pallas_call | solution.py:173
  133.3 48.6 %conditional.510 = (bf16[1040,256]{1,0:T(8,128)(2,1)}) conditional(s32[]{:T(128)} %convert_element_type.1548, (s32[]{:T(128)}, bf16[1040,256]{1,0:T(8,128)(2,1)}) %tuple.2562, (s32[]{:T(128)}, bf16[1040,256]{1,0:T(8,128)(2,1)}) %tuple.2562), branch_computations={%region_508.0_spmd, %region_635.0_spmd} | conditional | flops 18 | bytes 2130124 | solution.py:202
  142.6 30.7 %conditional.377 = (bf16[1040,256]{1,0:T(8,128)(2,1)}) conditional(s32[]{:T(128)} %convert_element_type.1410, (s32[]{:T(128)}, bf16[1040,256]{1,0:T(8,128)(2,1)}) %param.761, (s32[]{:T(128)}, bf16[1040,256]{1,0:T(8,128)(2,1)}) %param.761), branch_computations={%region_636.0_spmd, %region_699.0_spmd} | conditional | flops 15 | bytes 2130098 | solution.py:202
  143.2 29.6 %conditional.376 = (bf16[1040,256]{1,0:T(8,128)(2,1)}) conditional(s32[]{:T(128)} %convert_element_type.1409, (s32[]{:T(128)}, bf16[1040,256]{1,0:T(8,128)(2,1)}) %param.760, (s32[]{:T(128)}, bf16[1040,256]{1,0:T(8,128)(2,1)}) %param.760), branch_computations={%region_700.0_spmd, %region_731.0_spmd} | conditional | flops 12 | bytes 2130072 | solution.py:202
  149.0 23.8 %conditional.375 = (bf16[1040,256]{1,0:T(8,128)(2,1)}) conditional(s32[]{:T(128)} %convert_element_type.1408, (s32[]{:T(128)}, bf16[1040,256]{1,0:T(8,128)(2,1)}) %param.759, (s32[]{:T(128)}, bf16[1040,256]{1,0:T(8,128)(2,1)}) %param.759), branch_computations={%region_732.0_spmd, %region_747.0_spmd} | conditional | flops 9 | bytes 2130046 | solution.py:202
  149.6 23.2 %conditional.374 = (bf16[1040,256]{1,0:T(8,128)(2,1)}) conditional(s32[]{:T(128)} %convert_element_type.1407, (s32[]{:T(128)}, bf16[1040,256]{1,0:T(8,128)(2,1)}) %param.758, (s32[]{:T(128)}, bf16[1040,256]{1,0:T(8,128)(2,1)}) %param.758), branch_computations={%region_748.0_spmd, %region_755.0_spmd} | conditional | flops 6 | bytes 2130020 | solution.py:202
  150.2 22.6 %conditional.373 = (bf16[1040,256]{1,0:T(8,128)(2,1)}) conditional(s32[]{:T(128)} %convert_element_type.1406, (s32[]{:T(128)}, bf16[1040,256]{1,0:T(8,128)(2,1)}) %param.757, (s32[]{:T(128)}, bf16[1040,256]{1,0:T(8,128)(2,1)}) %param.757), branch_computations={%region_756.0_spmd, %region_759.0_spmd} | conditional | flops 3 | bytes 2129994 | solution.py:202
  150.9 22.0 %conditional.371 = (bf16[1040,256]{1,0:T(8,128)(2,1)}) conditional(s32[]{:T(128)} %convert_element_type.1404, bf16[1040,256]{1,0:T(8,128)(2,1)} %get-tuple-element.4614, bf16[1040,256]{1,0:T(8,128)(2,1)} %get-tuple-element.4614), branch_computations={%region_757.0_spmd, %region_758.0_spmd} | conditional | bytes 2129968 | solution.py:202
  152.2 20.7 %collective-permute-done.381 = bf16[1040,256]{1,0:T(8,128)(2,1)} collective-permute-done((bf16[1040,256]{1,0:T(8,128)(2,1)}, bf16[1040,256]{1,0:T(8,128)(2,1)}, u32[]{:S(2)}, u32[]{:S(2)}) %collective-permute-start.381) | collective-permute-done | bytes 532512 | tf_op jit(solution)/shard_map/cond/branch_1_fun/cond/branch_1_fun/cond/branch_1_fun/cond/branch_1_fun/cond/branch_1_fun/cond/branch_0_fun/cond/branch_1_fun/ppermute | solution.py:199
  183.1 9.6 %shard_map.62 = (f32[1024,256]{1,0:T(8,128)S(1)}, bf16[1040,256]{1,0:T(8,128)(2,1)}, bf16[1024,256]{1,0:T(8,128)(2,1)S(1)}) custom-call(s32[8]{0:T(128)S(1)} %get-tuple-element.4841.refs_1_.refs_0_.refs_11_, s32[8]{0:T(128)S(1)} %get-tuple-element.4842.refs_1_.refs_0_, f32[1024,256]{1,0:T(8,128)S(1)} %copy-done.5, ...), custom_call_target="tpu_custom_call" | custom-call | tf_op jit(solution)/shard_map/pallas_call | solution.py:173
  193.5 33.4 %conditional.511 = (bf16[1040,256]{1,0:T(8,128)(2,1)}) conditional(s32[]{:T(128)} %convert_element_type.1549, (s32[]{:T(128)}, bf16[1040,256]{1,0:T(8,128)(2,1)}) %tuple.2563, (s32[]{:T(128)}, bf16[1040,256]{1,0:T(8,128)(2,1)}) %tuple.2563), branch_computations={%region_762.0_spmd, %region_889.0_spmd} | conditional | flops 18 | bytes 2130124 | solution.py:202
  194.2 13.3 %conditional.440 = (bf16[1040,256]{1,0:T(8,128)(2,1)}) conditional(s32[]{:T(128)} %convert_element_type.1473, (s32[]{:T(128)}, bf16[1040,256]{1,0:T(8,128)(2,1)}) %param.888, (s32[]{:T(128)}, bf16[1040,256]{1,0:T(8,128)(2,1)}) %param.888), branch_computations={%region_763.0_spmd, %region_826.0_spmd} | conditional | flops 15 | bytes 2130098 | solution.py:202
  194.9 5.4 %conditional.408 = (bf16[1040,256]{1,0:T(8,128)(2,1)}) conditional(s32[]{:T(128)} %convert_element_type.1441, (s32[]{:T(128)}, bf16[1040,256]{1,0:T(8,128)(2,1)}) %param.824, (s32[]{:T(128)}, bf16[1040,256]{1,0:T(8,128)(2,1)}) %param.824), branch_computations={%region_764.0_spmd, %region_795.0_spmd} | conditional | flops 12 | bytes 2130072 | solution.py:202
  195.6 4.5 %conditional.392 = (bf16[1040,256]{1,0:T(8,128)(2,1)}) conditional(s32[]{:T(128)} %convert_element_type.1425, (s32[]{:T(128)}, bf16[1040,256]{1,0:T(8,128)(2,1)}) %param.792, (s32[]{:T(128)}, bf16[1040,256]{1,0:T(8,128)(2,1)}) %param.792), branch_computations={%region_765.0_spmd, %region_780.0_spmd} | conditional | flops 9 | bytes 2130046 | solution.py:202
  196.3 3.8 %conditional.384 = (bf16[1040,256]{1,0:T(8,128)(2,1)}) conditional(s32[]{:T(128)} %convert_element_type.1417, (s32[]{:T(128)}, bf16[1040,256]{1,0:T(8,128)(2,1)}) %param.776, (s32[]{:T(128)}, bf16[1040,256]{1,0:T(8,128)(2,1)}) %param.776), branch_computations={%region_766.0_spmd, %region_773.0_spmd} | conditional | flops 6 | bytes 2130020 | solution.py:202
  197.0 3.1 %conditional.380 = (bf16[1040,256]{1,0:T(8,128)(2,1)}) conditional(s32[]{:T(128)} %convert_element_type.1413, (s32[]{:T(128)}, bf16[1040,256]{1,0:T(8,128)(2,1)}) %param.768, (s32[]{:T(128)}, bf16[1040,256]{1,0:T(8,128)(2,1)}) %param.768), branch_computations={%region_767.0_spmd, %region_770.0_spmd} | conditional | flops 3 | bytes 2129994 | solution.py:202
  197.7 2.4 conditional.378
  198.0 2.1 collective-permute-done.385
  230.0 11.6 %shard_map.63 = (f32[1024,256]{1,0:T(8,128)}, bf16[16,256,256]{2,1,0:T(8,128)(2,1)S(1)}) custom-call(s32[8]{0:T(128)S(1)} %get-tuple-element.4842.refs_1_.refs_0_, f32[1024,256]{1,0:T(8,128)S(1)} %get-tuple-element.4831.refs_1_, bf16[1040,256]{1,0:T(8,128)(2,1)} %get-tuple-element.4832.refs_2_, bf16[1040,256]{1,0:T(8,128)(2,1)} %get-tuple-element.5355.refs_3_, ...), custom_call_target="tpu_custom_call" | custom-call | tf_op jit(solution)/shard_map/pallas_call | solution.py:173
  243.3 2.4 collective-permute-done.512
  247.3 21.0 %all_to_all.10 = bf16[64,32,256]{2,1,0:T(8,128)(2,1)S(1)} all-to-all(bf16[64,32,256]{2,1,0:T(8,128)(2,1)S(1)} %bitcast.27), channel_id=1, replica_groups=mesh['group'=8,'member'=16] {'group','member':(1)8}, dimensions={0} | all-to-all | bytes 2097152 | tf_op jit(solution)/shard_map/all_to_all | solution.py:217
  268.5 23.1 %all_to_all.11 = bf16[64,32,256]{2,1,0:T(8,128)(2,1)S(1)} all-to-all(bf16[64,32,256]{2,1,0:T(8,128)(2,1)S(1)} %broadcast_in_dim.2), channel_id=1, replica_groups=mesh['group'=8,'member'=16] {'group','member':(1)8}, dimensions={0} | all-to-all | bytes 2097152 | tf_op jit(solution)/shard_map/all_to_all | solution.py:219
  291.6 1.5 collective-permute-start.513
  293.1 2.3 collective-permute-done.513
  295.5 2.0 copy-done.1
  297.6 2.6 multiply_subtract_fusion
  (37 shorter events, 15.1 us)
Async XLA Ops:
  0.6 49.3 %copy-start.2 = (f32[1024,256]{1,0:T(8,128)S(1)}, f32[1024,256]{1,0:T(8,128)}, u32[]{:S(2)}) copy-start(f32[1024,256]{1,0:T(8,128)} %refs_2_.1) | copy-start | bytes 3145732
  2.0 48.0 %copy-start.14 = (s32[8]{0:T(128)S(1)}, s32[8]{0:T(128)}, u32[]{:S(2)}) copy-start(s32[8]{0:T(128)} %get-tuple-element.4840.rel_ref.refs_0_.refs_5_) | copy-start | bytes 100
  10.7 18.4 %collective-permute-start.15 = (bf16[1040,256]{1,0:T(8,128)(2,1)}, bf16[1040,256]{1,0:T(8,128)(2,1)}, u32[]{:S(2)}, u32[]{:S(2)}) collective-permute-start(bf16[1040,256]{1,0:T(8,128)(2,1)} %param.26), channel_id=1, source_target_pairs={{0,15},{1,14},{2,13},{3,12},{4,11},{5,10},{6,9},{7,8},{8,7},{9,6},... | collective-permute-start | bytes 1597448 | tf_op jit(solution)/shard_map/cond/branch_0_fun/cond/branch_0_fun/cond/branch_0_fun/cond/branch_1_fun/cond/branch_1_fun/cond/branch_1_fun/cond/branch_1_fun/ppermute | solution.py:199
  50.0 2.2 copy-start
  62.1 1.0 copy-start.6
  63.0 0.8 copy-start.8
  63.8 57.4 %copy-start.7 = (f32[1024,256]{1,0:T(8,128)S(1)}, f32[1024,256]{1,0:T(8,128)}, u32[]{:S(2)}) copy-start(f32[1024,256]{1,0:T(8,128)} %copy-done.6) | copy-start | bytes 3145732
  82.4 29.6 %collective-permute-start.255 = (bf16[1040,256]{1,0:T(8,128)(2,1)}, bf16[1040,256]{1,0:T(8,128)(2,1)}, u32[]{:S(2)}, u32[]{:S(2)}) collective-permute-start(bf16[1040,256]{1,0:T(8,128)(2,1)} %param.501), channel_id=1, source_target_pairs={{0,127},{1,126},{2,125},{3,124},{4,123},{5,122},{6,121},{7,120},{8... | collective-permute-start | bytes 1597448 | tf_op jit(solution)/shard_map/cond/branch_1_fun/cond/branch_1_fun/cond/branch_1_fun/cond/branch_1_fun/cond/branch_1_fun/cond/branch_1_fun/cond/branch_1_fun/ppermute | solution.py:199
  130.8 1.0 copy-start.4
  131.8 0.8 copy-start.10
  150.9 22.0 %collective-permute-start.381 = (bf16[1040,256]{1,0:T(8,128)(2,1)}, bf16[1040,256]{1,0:T(8,128)(2,1)}, u32[]{:S(2)}, u32[]{:S(2)}) collective-permute-start(bf16[1040,256]{1,0:T(8,128)(2,1)} %param.752), channel_id=1, source_target_pairs={{0,125},{1,124},{2,127},{3,126},{4,121},{5,120},{6,123},{7,122},{8... | collective-permute-start | bytes 1597448 | tf_op jit(solution)/shard_map/cond/branch_1_fun/cond/branch_1_fun/cond/branch_1_fun/cond/branch_1_fun/cond/branch_1_fun/cond/branch_0_fun/cond/branch_1_fun/ppermute | solution.py:199
  181.9 1.2 copy-start.5
  192.7 0.8 copy-start.12
  197.7 2.3 collective-permute-start.385
  226.9 1.0 copy-start.9
  227.9 1.0 copy-start.11
  229.0 1.0 copy-start.13
  241.6 1.3 copy-start.3
  243.0 2.7 collective-permute-start.512
  291.6 3.8 %collective-permute-start.513 = (bf16[8,256,256]{2,1,0:T(8,128)(2,1)S(1)}, bf16[8,256,256]{2,1,0:T(8,128)(2,1)S(1)}, u32[]{:S(2)}, u32[]{:S(2)}) collective-permute-start(bf16[8,256,256]{2,1,0:T(8,128)(2,1)S(1)} %bitcast.25), channel_id=1, source_target_pairs={{0,1},{1,0},{2,3},{3,2},{4,5},{5,4},{6,7},{7,6},{8,9},{9,8},{10,11... | collective-permute-start | bytes 3145736 | tf_op jit(solution)/shard_map/ppermute | solution.py:221
  295.4 2.2 copy-start.1
